TPU v7x, 256 devices: a whole 4x4x8 slice. The times are simulated.
256 devices in a mesh: term: 16 (over z_lo, x), space: 16 (over y, z_hi, core).
Axes of the slice: x: 4, y: 4, z: 8 (z_hi: 2, z_lo: 4; z = z_hi * 4 + z_lo), core: 2. Of those that a mesh axis runs over, the one named last changes fastest.
Arguments:
- fields: float32 [288, 512, 256], P('term', 'space'), may hold values from -6 to 6
- modes: float32 [11, 512, 256], P(None, 'space'), may hold values from -6 to 6
- pair_list: int32 [2048, 3], replicated, may hold values from 0 to 287, as said below
- pair_value: float32 [2048], replicated, may hold values from -2 to 2
- assign: int32 [288], replicated, may hold values from 0 to 287, each once
Outputs:
- result: float32 [288, 512, 256], P('term', 'space')
Inputs may be any that keep to these rules, and one draw needn't show every extreme that they name: `pair_list`: terms are the multi-indices of total degree 3 or less over 11 - 1 variables in graded order, the first 288 of them, terms beyond the 286 such indices having none. Every term t has a row (t, t, 0); for each term alpha and variable v whose index alpha + e_v is also a term u there are rows (alpha, u, v + 1) and (u, alpha, v + 1); these rows stand once each, and the remaining rows repeat diagonal rows (t, t, 0). Rows are in random order.
All inputs are finite; a program needn't handle non-finite values.
Results may differ from a plain program's by a relative error of at most 0.00012.
Values sent between devices are 32-bit elements; how exact they have to be, the bound alone decides.
No kernel may reach another device: no remote copies, remote signals or barrier semaphores. Data moves between devices by JAX's collectives and lax.ppermute only.
A program may use at most 64 MiB of HBM per device.

v0:
```python
import functools

import jax
import jax.numpy as jnp
from jax import lax
from jax.experimental import pallas as pl
from jax.experimental.pallas import tpu as pltpu
from jax.sharding import PartitionSpec as P

PAIRS = 9
ROWS = 96
TOP = 72
BOTTOM = 81
SIDE = 90
LOWER = 66
VARS = 10


def lanes_of(shape=(8, 128)):
    return lax.broadcasted_iota(jnp.int32, shape, 1)


def subs_of(shape=(8, 128)):
    return lax.broadcasted_iota(jnp.int32, shape, 0)


def pack_kernel(f_ref, out_ref):
    lane, sub = lanes_of(), subs_of()
    low = lane < 64
    even = lane % 2 == 0
    spare = lane % 64 >= 32
    for r in range(4):
        near, far = [], []
        for h in range(2):
            ga = jnp.zeros((8, 128), jnp.float32)
            gb = jnp.zeros((8, 128), jnp.float32)
            for p in range(PAIRS):
                a = f_ref[p, pl.ds(8 * r, 8), pl.ds(128 * h, 128)]
                b = f_ref[p + PAIRS, pl.ds(8 * r, 8), pl.ds(128 * h, 128)]
                both = (
                    jnp.where(low, a, pltpu.roll(b, 64, 1)),
                    jnp.where(low, pltpu.roll(a, 64, 1), b),
                )
                for o in range(2):
                    c = 2 * h + o
                    out_ref[4 * r + c, pl.ds(8 * p, 8), :] = both[o]
                    if r < 3:
                        out_ref[4 * (r + 1) + c, pl.ds(TOP + p, 1), :] = both[o][7:8]
                    if r > 0:
                        out_ref[4 * (r - 1) + c, pl.ds(BOTTOM + p, 1), :] = both[o][0:1]
                here = (lane % 64) // 2 == p
                ga = jnp.where(here, pltpu.roll(a, (2 * p - 63) % 128, 1), ga)
                gb = jnp.where(here, pltpu.roll(b, 2 * p + 1, 1), gb)
            near.append(jnp.where(low, ga, gb))
            far.append(pltpu.roll(jnp.where(low, gb, ga), 64, 1))
        zero = jnp.zeros((8, 128), jnp.float32)
        sides = (
            jnp.where(even, zero, near[0]),
            jnp.where(even, near[0], far[1]),
            jnp.where(even, far[0], near[1]),
            jnp.where(even, near[1], zero),
        )
        for c in range(4):
            moved = pltpu.roll(pltpu.roll(sides[c], 32, 1), 2, 0)
            kept = jnp.where(spare, moved, sides[c])
            out_ref[4 * r + c, pl.ds(SIDE, 6), :] = kept[0:6]


def edge_kernel(place_ref, sent_ref, above_ref, below_ref, modes_ref, out_ref, coef_ref):
    lane, sub = lanes_of(), subs_of()
    low = lane < 64
    low9 = lanes_of((PAIRS, 128)) < 64
    out_ref[...] = sent_ref[...]

    def place(ref, row):
        for h in range(2):
            a = ref[pl.ds(0, PAIRS), pl.ds(128 * h, 128)]
            b = ref[pl.ds(PAIRS, PAIRS), pl.ds(128 * h, 128)]
            out_ref[2 * h, pl.ds(row, PAIRS), :] = jnp.where(low9, a, pltpu.roll(b, 64, 1))
            out_ref[2 * h + 1, pl.ds(row, PAIRS), :] = jnp.where(low9, pltpu.roll(a, 64, 1), b)

    @pl.when(pl.program_id(0) == 0)
    def _():
        place(above_ref, 0)
        block_row = place_ref[0] // 4
        block_col = place_ref[0] % 4
        first = block_row == 0
        last = block_row == 3
        odd = block_col % 2 == 1
        right_half = block_col >= 2
        wide_lane = lanes_of((8, 256))
        wide_sub = subs_of((8, 256))
        count = modes_ref.shape[0]

        def one(k, carry):
            here = modes_ref[k, pl.ds(pl.multiple_of(8 * block_row, 8), 8), :]
            before = modes_ref[k, pl.ds(pl.multiple_of(8 * jnp.maximum(block_row - 1, 0), 8), 8), :]
            after = modes_ref[k, pl.ds(pl.multiple_of(8 * jnp.minimum(block_row + 1, 3), 8), 8), :]
            over = jnp.where(first, above_ref[pl.ds(2 * PAIRS + k, 1), :], before[7:8])
            under = jnp.where(last, below_ref[pl.ds(2 * PAIRS + k, 1), :], after[0:1])
            up = jnp.where(wide_sub == 0, over, pltpu.roll(here, 1, 0))
            down = jnp.where(wide_sub == 7, under, pltpu.roll(here, 7, 0))
            left = jnp.where(wide_lane == 0, 0.0, pltpu.roll(here, 1, 1))
            right = jnp.where(wide_lane == 255, 0.0, pltpu.roll(here, 255, 1))

            def both(x, y):
                x = 0.5 * (here + x)
                y = 0.5 * (here + y)
                x = jnp.where(right_half, x[:, 128:], x[:, :128])
                y = jnp.where(right_half, y[:, 128:], y[:, :128])
                return jnp.where(
                    odd,
                    jnp.where(low, pltpu.roll(x, 64, 1), y),
                    jnp.where(low, x, pltpu.roll(y, 64, 1)),
                )

            coef_ref[k, pl.ds(0, 8), :] = both(up, down)
            coef_ref[k, pl.ds(8, 8), :] = both(left, right)
            return carry

        lax.fori_loop(0, count, one, 0)

    @pl.when(pl.program_id(0) == 1)
    def _():
        place(below_ref, PAIRS)


def mix_kernel(assign_ref, upper_ref, weight_ref, got_ref, coef_ref, out_ref, diff, total):
    lane, sub = lanes_of(), subs_of()
    low = lane < 64

    def load(group, carry):
        tail = got_ref[group, pl.ds(ROWS - 8, 8), :]
        beside = jnp.where(
            sub < 6, pltpu.roll(tail, 6, 0), pltpu.roll(pltpu.roll(tail, 96, 1), 4, 0)
        )
        coef_v = coef_ref[0, pl.ds(0, 8), :]
        coef_h = coef_ref[0, pl.ds(8, 8), :]
        for p in range(PAIRS):
            here = got_ref[group, pl.ds(8 * p, 8), :]
            up = jnp.where(sub == 0, got_ref[group, pl.ds(TOP + p, 1), :], pltpu.roll(here, 1, 0))
            down = jnp.where(sub == 7, got_ref[group, pl.ds(BOTTOM + p, 1), :], pltpu.roll(here, 7, 0))
            left = jnp.where(
                lane % 64 == 0, pltpu.roll(beside, (128 - 2 * p) % 128, 1), pltpu.roll(here, 1, 1)
            )
            right = jnp.where(
                lane % 64 == 63, pltpu.roll(beside, 62 - 2 * p, 1), pltpu.roll(here, 127, 1)
            )
            up, down, left, right = here - up, here - down, here - left, here - right
            for o in range(2):
                term = assign_ref[group * (2 * PAIRS) + o * PAIRS + p]
                if o == 0:
                    vert = jnp.where(low, up, pltpu.roll(down, 64, 1))
                    hori = jnp.where(low, left, pltpu.roll(right, 64, 1))
                else:
                    vert = jnp.where(low, pltpu.roll(up, 64, 1), down)
                    hori = jnp.where(low, pltpu.roll(left, 64, 1), right)
                diff[term, pl.ds(0, 8), :] = vert
                diff[term, pl.ds(8, 8), :] = hori
                total[term] = weight_ref[0, term] * (coef_v * vert + coef_h * hori)
        return carry

    lax.fori_loop(0, got_ref.shape[0], load, 0)

    def couple(term, carry):
        vert = diff[term, pl.ds(0, 8), :]
        hori = diff[term, pl.ds(8, 8), :]
        own = total[term]
        uppers = [upper_ref[v, term] for v in range(VARS)]
        sums = [total[upper] for upper in uppers]
        for v in range(VARS):
            coef_v = coef_ref[v + 1, pl.ds(0, 8), :]
            coef_h = coef_ref[v + 1, pl.ds(8, 8), :]
            upper = uppers[v]
            own = own + weight_ref[1 + v, term] * (
                coef_v * diff[upper, pl.ds(0, 8), :] + coef_h * diff[upper, pl.ds(8, 8), :]
            )
            sums[v] = sums[v] + weight_ref[1 + VARS + v, term] * (coef_v * vert + coef_h * hori)
        total[term] = own
        for v in range(VARS):
            total[uppers[v]] = sums[v]
        return carry

    lax.fori_loop(0, LOWER, couple, 0)

    def store(group, carry):
        for p in range(PAIRS):
            a = total[assign_ref[group * (2 * PAIRS) + p]]
            b = total[assign_ref[group * (2 * PAIRS) + PAIRS + p]]
            out_ref[group, pl.ds(8 * p, 8), :] = jnp.where(
                low, a + pltpu.roll(a, 64, 1), b + pltpu.roll(b, 64, 1)
            )
        return carry

    lax.fori_loop(0, got_ref.shape[0], store, 0)


def unpack_kernel(got_ref, out_ref):
    low = lanes_of() < 64
    for r in range(4):
        for h in range(2):
            for p in range(PAIRS):
                one = got_ref[4 * r + 2 * h, pl.ds(8 * p, 8), :]
                two = got_ref[4 * r + 2 * h + 1, pl.ds(8 * p, 8), :]
                out_ref[p, pl.ds(8 * r, 8), pl.ds(128 * h, 128)] = jnp.where(
                    low, one, pltpu.roll(two, 64, 1)
                )
                out_ref[p + PAIRS, pl.ds(8 * r, 8), pl.ds(128 * h, 128)] = jnp.where(
                    low, pltpu.roll(one, 64, 1), two
                )


def vmem():
    return pl.BlockSpec(memory_space=pltpu.VMEM)


def smem():
    return pl.BlockSpec(memory_space=pltpu.SMEM)


def f32(*shape):
    return jax.ShapeDtypeStruct(shape, jnp.float32)


PARAMS = pltpu.CompilerParams(vmem_limit_bytes=32 * 1024 * 1024)


def pack(fields, groups):
    return pl.pallas_call(
        pack_kernel,
        out_shape=f32(groups, ROWS, 128),
        in_specs=[vmem()],
        out_specs=vmem(),
        compiler_params=PARAMS,
        cost_estimate=pl.CostEstimate(flops=10**6, bytes_accessed=1400000, transcendentals=0),
    )(fields)


def edges(place, sent, above, below, modes):
    count = modes.shape[0]
    part = pl.BlockSpec((4, 24, 128), lambda i: (3 * i, 3, 0))
    whole = lambda x: pl.BlockSpec(x.shape, lambda i: (0,) * x.ndim)
    return pl.pallas_call(
        edge_kernel,
        grid=(2,),
        out_shape=(f32(*sent.shape), f32(count, 16, 128)),
        in_specs=[smem(), part, whole(above), whole(below), whole(modes)],
        out_specs=(part, pl.BlockSpec((count, 16, 128), lambda i: (0, 0, 0))),
        input_output_aliases={1: 0},
        compiler_params=PARAMS,
    )(place, sent, above, below, modes)


def mix(assign, uppers, weights, got, coef):
    groups = got.shape[0]
    return pl.pallas_call(
        mix_kernel,
        out_shape=f32(groups, 8 * PAIRS, 128),
        in_specs=[smem(), smem(), smem(), vmem(), vmem()],
        out_specs=vmem(),
        scratch_shapes=[
            pltpu.VMEM((groups * 2 * PAIRS, 16, 128), jnp.float32),
            pltpu.VMEM((groups * 2 * PAIRS, 8, 128), jnp.float32),
        ],
        compiler_params=PARAMS,
    )(assign, uppers, weights, got, coef)


def unpack(got, shape):
    return pl.pallas_call(
        unpack_kernel,
        out_shape=f32(*shape),
        in_specs=[vmem()],
        out_specs=vmem(),
        compiler_params=PARAMS,
    )(got)


def tables(pair_list, pair_value, terms, mode_count):
    row, col, mode = pair_list[:, 0], pair_list[:, 1], pair_list[:, 2]
    at = (jnp.minimum(row, col)[:, None] == jnp.arange(terms, dtype=jnp.int32)[None, :]).astype(jnp.float32)
    kinds = jnp.arange(1 + 3 * VARS, dtype=jnp.int32)[:, None]
    wanted = jnp.where(kinds <= VARS, kinds, (kinds - 1) % VARS + 1)
    side = jnp.where(
        kinds <= VARS, row <= col, jnp.where(kinds <= 2 * VARS, row > col, row < col)
    )
    value = jnp.where(kinds <= 2 * VARS, pair_value, col.astype(jnp.float32))
    value = jnp.where((mode[None, :] == wanted) & side, value, 0.0)
    found = jnp.dot(value, at, precision=lax.Precision.HIGHEST, preferred_element_type=jnp.float32)
    uppers = jnp.round(found[1 + 2 * VARS :]).astype(jnp.int32)
    return found[: 1 + 2 * VARS], uppers


def shards(fields, modes, pair_list, pair_value, assign):
    groups = lax.axis_size("term")
    count = lax.axis_size("space")
    ends = count - 1
    last = fields.shape[1] - 1
    head = jnp.concatenate([fields[:, 0], modes[:, 0]], axis=0)
    tail = jnp.concatenate([fields[:, last], modes[:, last]], axis=0)
    above = lax.ppermute(tail, "space", [(i, i + 1) for i in range(ends)])
    below = lax.ppermute(head, "space", [(i + 1, i) for i in range(ends)])
    weights, uppers = tables(pair_list, pair_value, groups * fields.shape[0], modes.shape[0])
    sent = pack(fields, groups)
    place = lax.axis_index("term").astype(jnp.int32).reshape(1)
    sent, coef = edges(place, sent, above, below, modes)
    got = lax.all_to_all(sent, "term", 0, 0, tiled=True)
    mixed = mix(assign, uppers, weights, got, coef)
    back = lax.all_to_all(mixed, "term", 0, 0, tiled=True)
    return unpack(back, fields.shape)


def solution(mesh):
    return jax.shard_map(
        shards,
        mesh=mesh,
        in_specs=(P("term", "space", None), P(None, "space", None), P(), P(), P()),
        out_specs=P("term", "space", None),
        check_vma=False,
    )
```

profile of v0, /device:TPU:16, one launch (start us, length us, event | category | flops | bytes accessed | tf_op | source)
XLA Modules:
  0.0 82.5 jit_solution(2610344330769510265)
XLA Ops:
  0.0 1.0 %fusion.23 = (f32[11,1,256]{2,1,0:T(1,128)S(1)}, f32[11,1,256]{2,1,0:T(1,128)S(1)}) fusion(f32[11,32,256]{2,1,0:T(8,128)} %modes_ref.1), kind=kLoop, calls=%fused_computation.41 | loop fusion | bytes 45056 | tf_op jit(solution)/shard_map/slice | solution.py:299
  1.0 0.0 copy-start.1
  1.0 1.1 %fusion.22 = (f32[18,1,256]{2,1,0:T(1,128)S(1)}, f32[18,1,256]{2,1,0:T(1,128)S(1)}) fusion(f32[18,32,256]{2,1,0:T(8,128)} %f_ref.1), kind=kLoop, calls=%fused_computation.40 | loop fusion | bytes 73728 | tf_op jit(solution)/shard_map/slice | solution.py:299
  2.1 1.9 %collective-permute-start = (f32[29,256]{1,0:T(8,128)S(1)}, f32[29,256]{1,0:T(8,128)S(1)}, u32[]{:S(2)}, u32[]{:S(2)}) collective-permute-start(f32[29,256]{1,0:T(8,128)S(1)} %pad_maximum_fusion), channel_id=1, source_target_pairs={{0,1},{1,2},{2,3},{3,4},{4,5},{5,6},{6,7},{7,8},{8,9},{9,10},{10,1... | collective-permute-start | bytes 89096 | tf_op jit(solution)/shard_map/ppermute | solution.py:301
  4.0 8.4 %collective-permute-start.1 = (f32[29,256]{1,0:T(8,128)S(1)}, f32[29,256]{1,0:T(8,128)S(1)}, u32[]{:S(2)}, u32[]{:S(2)}) collective-permute-start(f32[29,256]{1,0:T(8,128)S(1)} %pad_maximum_fusion.1), channel_id=1, source_target_pairs={{1,0},{2,1},{3,2},{4,3},{5,4},{6,5},{7,6},{8,7},{9,8},{10,9},{11,1... | collective-permute-start | bytes 89096 | tf_op jit(solution)/shard_map/ppermute | solution.py:302
  12.5 0.0 copy-start
  12.5 1.1 %copy-done = f32[18,32,256]{2,1,0:T(8,128)S(1)} copy-done((f32[18,32,256]{2,1,0:T(8,128)S(1)}, f32[18,32,256]{2,1,0:T(8,128)}, u32[]{:S(2)}) %copy-start) | copy-done | bytes 589848
  13.6 1.8 %shard_map.55.sent_ref = f32[16,96,128]{2,1,0:T(8,128)} custom-call(f32[18,32,256]{2,1,0:T(8,128)S(1)} %copy-done), custom_call_target="tpu_custom_call" | custom-call | flops 1000000 | bytes 1400000 | tf_op jit(solution)/shard_map/pallas_call | solution.py:229
  15.3 0.0 collective-permute-done.above_ref
  15.3 0.0 collective-permute-done.1.below_ref
  15.3 0.0 copy-done.1
  15.3 3.2 %shard_map.56 = (f32[16,96,128]{2,1,0:T(8,128)}, f32[11,16,128]{2,1,0:T(8,128)S(1)}) custom-call(s32[1]{0:T(128)} %bitcast.3.place_ref, f32[16,96,128]{2,1,0:T(8,128)} %shard_map.55.sent_ref, f32[29,256]{1,0:T(8,128)S(1)} %collective-permute-done.above_ref, f32[29,256]{1,0:T(8,128)S(1)} %collective-permute-done.1.below_ref, ...), custom_call_target="tpu_custom_call", output_to_operand_aliasing={{0}: (1, {})} | custom-call | tf_op jit(solution)/shard_map/pallas_call | solution.py:243
  18.6 0.0 copy-start.3
  18.6 8.6 %all-to-all-start = ((f32[16,96,128]{2,1,0:T(8,128)}), f32[16,96,128]{2,1,0:T(8,128)S(1)}, u32[]{:S(2)}, u32[]{:S(2)}) async-start(f32[16,96,128]{2,1,0:T(8,128)} %get-tuple-element.7), calls=%async_computation | async-start | bytes 1572864 | tf_op jit(solution)/shard_map/all_to_all | solution.py:307
  27.2 0.0 copy-done.3
  27.2 0.1 compare_reduce_fusion.2
  27.3 0.0 copy-done.4
  27.3 0.0 copy-start.2
  27.3 1.3 %fusion = f32[31,288]{1,0:T(8,128)S(1)} fusion(s32[2048]{0:T(1024)S(1)} %bitcast.21, f32[2048]{0:T(1024)S(1)} %bitcast.22, f32[2048]{0:T(1024)S(1)} %copy-done.4, s32[2048]{0:T(1024)S(1)} %bitcast.20, s32[31]{0:T(128)S(1)} %iota_select_fusion, pred[31]{0:T(512)(128)(4,1)S(1)} %get-tuple-element.19, pred[2048]{0:T(1024)(128)(4,1)S(1)} %get-tuple-element.11, ...), kind=kOutput, calls=%fused_computation.1 | convolution fusion | flops 220385280 | bytes 74810 | tf_op jit(solution)/shard_map/dot_general | solution.py:289
  28.7 18.0 %all-to-all-done.got_ref = f32[16,96,128]{2,1,0:T(8,128)S(1)} async-done(((f32[16,96,128]{2,1,0:T(8,128)}), f32[16,96,128]{2,1,0:T(8,128)S(1)}, u32[]{:S(2)}, u32[]{:S(2)}) %all-to-all-start) | async-done | bytes 786464 | tf_op jit(solution)/shard_map/all_to_all | solution.py:307
  46.7 0.0 copy-done.2
  46.7 9.8 %shard_map.57 = f32[16,72,128]{2,1,0:T(8,128)S(1)} custom-call(s32[288]{0:T(512)S(1)} %copy-done.2, s32[10,288]{1,0:T(8,128)S(1)} %fusion.18.upper_ref, f32[21,288]{1,0:T(8,128)S(1)} %slice.37.weight_ref, f32[16,96,128]{2,1,0:T(8,128)S(1)} %all-to-all-done.got_ref, f32[11,16,128]{2,1,0:T(8,128)S(1)} %get-tuple-element.8.coef_ref), custom_call_target="tpu_custom_call" | custom-call | tf_op jit(solution)/shard_map/pallas_call | solution.py:256
  56.6 24.9 %all_to_all.10.got_ref = f32[16,72,128]{2,1,0:T(8,128)S(1)} all-to-all(f32[16,72,128]{2,1,0:T(8,128)S(1)} %shard_map.57), channel_id=1, replica_groups=mesh['term'=16,'space'=16] {'term'}, dimensions={0} | all-to-all | bytes 1179648 | tf_op jit(solution)/shard_map/all_to_all | solution.py:309
  81.5 1.0 %shard_map.58 = f32[18,32,256]{2,1,0:T(8,128)} custom-call(f32[16,72,128]{2,1,0:T(8,128)S(1)} %all_to_all.10.got_ref), custom_call_target="tpu_custom_call" | custom-call | tf_op jit(solution)/shard_map/pallas_call | solution.py:270
  (12 shorter events, 0.1 us)
Async XLA Ops:
  1.0 14.4 %copy-start.1 = (f32[11,32,256]{2,1,0:T(8,128)S(1)}, f32[11,32,256]{2,1,0:T(8,128)}, u32[]{:S(2)}) copy-start(f32[11,32,256]{2,1,0:T(8,128)} %modes_ref.1) | copy-start | bytes 1081348
  2.1 13.3 %collective-permute-start = (f32[29,256]{1,0:T(8,128)S(1)}, f32[29,256]{1,0:T(8,128)S(1)}, u32[]{:S(2)}, u32[]{:S(2)}) collective-permute-start(f32[29,256]{1,0:T(8,128)S(1)} %pad_maximum_fusion), channel_id=1, source_target_pairs={{0,1},{1,2},{2,3},{3,4},{4,5},{5,6},{6,7},{7,8},{8,9},{9,10},{10,1... | collective-permute-start | bytes 89096 | tf_op jit(solution)/shard_map/ppermute | solution.py:301
  4.0 11.3 %collective-permute-start.1 = (f32[29,256]{1,0:T(8,128)S(1)}, f32[29,256]{1,0:T(8,128)S(1)}, u32[]{:S(2)}, u32[]{:S(2)}) collective-permute-start(f32[29,256]{1,0:T(8,128)S(1)} %pad_maximum_fusion.1), channel_id=1, source_target_pairs={{1,0},{2,1},{3,2},{4,3},{5,4},{6,5},{7,6},{8,7},{9,8},{10,9},{11,1... | collective-permute-start | bytes 89096 | tf_op jit(solution)/shard_map/ppermute | solution.py:302
  12.5 1.1 %copy-start = (f32[18,32,256]{2,1,0:T(8,128)S(1)}, f32[18,32,256]{2,1,0:T(8,128)}, u32[]{:S(2)}) copy-start(f32[18,32,256]{2,1,0:T(8,128)} %f_ref.1) | copy-start | bytes 1769476
  18.6 8.6 %copy-start.3 = (s32[2048,3]{0,1:T(4,128)S(1)}, s32[2048,3]{0,1:T(4,128)}, u32[]{:S(2)}) copy-start(s32[2048,3]{0,1:T(4,128)} %param.7) | copy-start | bytes 73732
  18.6 8.8 %copy-start.4 = (f32[2048]{0:T(1024)S(1)}, f32[2048]{0:T(1024)}, u32[]{:S(2)}) copy-start(f32[2048]{0:T(1024)} %param.8) | copy-start | bytes 24580
  18.6 28.1 %all-to-all-start = ((f32[16,96,128]{2,1,0:T(8,128)}), f32[16,96,128]{2,1,0:T(8,128)S(1)}, u32[]{:S(2)}, u32[]{:S(2)}) async-start(f32[16,96,128]{2,1,0:T(8,128)} %get-tuple-element.7), calls=%async_computation | async-start | bytes 1572864 | tf_op jit(solution)/shard_map/all_to_all | solution.py:307
  27.3 19.4 %copy-start.2 = (s32[288]{0:T(512)S(1)}, s32[288]{0:T(512)}, u32[]{:S(2)}) copy-start(s32[288]{0:T(512)} %assign_ref.1) | copy-start | bytes 3460
where the time goes:
time: 83 us; the launch traced here: 82.5 us
  blocking collectives  24.9 us (30%)
  starting transfers between devices  19 us (23%)
  waiting for transfers between devices  18 us (22%)
  Pallas kernels  15.9 us (19%)
  local copies, waits for them, and re-layouts  3.11 us (4%)
  matrix products  1.29 us (2%)
    all_to_all x1, blocking collectives, shards(): back = lax.all_to_all(mixed, 'term', 0, 0, tiled=True)  24.9 us
    all_to_all x1, waiting for transfers between devices, shards(): got = lax.all_to_all(sent, 'term', 0, 0, tiled=True)  18 us
    pallas_call x1, Pallas kernels, mix(): pl.pallas_call(mix_kernel, out_shape=f32(groups, 8 * PAIRS, 128), in_spec...  9.85 us
    all_to_all x1, starting transfers between devices, shards(): got = lax.all_to_all(sent, 'term', 0, 0, tiled=True)  8.6 us
    ppermute x1, starting transfers between devices, shards(): below = lax.ppermute(head, 'space', [(i + 1, i) for i in range(ends)])  8.45 us
    pallas_call x1, Pallas kernels, edges(): pl.pallas_call(edge_kernel, grid=(2,), out_shape=(f32(*sent.shape), f32(c...  3.22 us
    slice x2, local copies, waits for them, and re-layouts, shards(): head = jnp.concatenate([fields[:, 0], modes[:, 0]], axis=0)  2.01 us
    ppermute x1, starting transfers between devices, shards(): above = lax.ppermute(tail, 'space', [(i, i + 1) for i in range(ends)])  1.92 us
  transfers between devices with their start and end apart: 3, of which 1 were waited for; matrix products, arithmetic and copies ran while one was open for 2% of the time, Pallas kernels for 2%

commit v1 on v0

v1 whole, which is shorter than its diff:
```python
import jax
import jax.numpy as jnp
from jax import lax
from jax.experimental import pallas as pl
from jax.experimental.pallas import tpu as pltpu
from jax.sharding import PartitionSpec as P

PAIRS = 9
BLOCK = 8 * PAIRS
ROWS = 96
FIRST = 72
SECOND = 81
SIDE = 90
LOWER = 66
VARS = 10


def holder(r, c):
    return 4 * c + (r ^ c)


def row_group(place):
    return (place & 3) ^ (place >> 2)


def lanes_of(shape=(8, 128)):
    return lax.broadcasted_iota(jnp.int32, shape, 1)


def subs_of(shape=(8, 128)):
    return lax.broadcasted_iota(jnp.int32, shape, 0)


def pack_kernel(f_ref, out_ref):
    lane = lanes_of()
    low = lane < 64
    even = lane % 2 == 0
    spare = lane % 64 >= 32
    for r in range(4):
        near, far = [], []
        for h in range(2):
            ga = jnp.zeros((8, 128), jnp.float32)
            gb = jnp.zeros((8, 128), jnp.float32)
            for p in range(PAIRS):
                a = f_ref[p, pl.ds(8 * r, 8), pl.ds(128 * h, 128)]
                b = f_ref[p + PAIRS, pl.ds(8 * r, 8), pl.ds(128 * h, 128)]
                both = (
                    jnp.where(low, a, pltpu.roll(b, 64, 1)),
                    jnp.where(low, pltpu.roll(a, 64, 1), b),
                )
                for o in range(2):
                    c = 2 * h + o
                    first, last = both[o][0:1], both[o][7:8]
                    out_ref[holder(r, c), pl.ds(8 * p, 8), :] = both[o]
                    if r == 0:
                        out_ref[holder(0, c), pl.ds(FIRST + p, 1), :] = first
                    if r == 3:
                        out_ref[holder(3, c), pl.ds(FIRST + p, 1), :] = last
                    if r < 3:
                        out_ref[holder(r + 1, c), pl.ds((FIRST if r < 2 else SECOND) + p, 1), :] = last
                    if r > 0:
                        out_ref[holder(r - 1, c), pl.ds(SECOND + p, 1), :] = first
                here = (lane % 64) // 2 == p
                ga = jnp.where(here, pltpu.roll(a, (2 * p - 63) % 128, 1), ga)
                gb = jnp.where(here, pltpu.roll(b, 2 * p + 1, 1), gb)
            near.append(jnp.where(low, ga, gb))
            far.append(pltpu.roll(jnp.where(low, gb, ga), 64, 1))
        zero = jnp.zeros((8, 128), jnp.float32)
        sides = (
            jnp.where(even, zero, near[0]),
            jnp.where(even, near[0], far[1]),
            jnp.where(even, far[0], near[1]),
            jnp.where(even, near[1], zero),
        )
        for c in range(4):
            moved = pltpu.roll(pltpu.roll(sides[c], 32, 1), 2, 0)
            kept = jnp.where(spare, moved, sides[c])
            out_ref[holder(r, c), pl.ds(SIDE, 6), :] = kept[0:6]


def edge_kernel(got_ref, edge_ref):
    groups = got_ref.shape[0]
    for group in range(groups):
        edge_ref[pl.ds(8 * group, 8), :] = got_ref[group, pl.ds(FIRST, 8), :]
        edge_ref[pl.ds(8 * groups + group, 1), :] = got_ref[group, pl.ds(FIRST + 8, 1), :]


def coef_kernel(place_ref, modes_ref, edge_ref, coef_ref):
    low = lanes_of() < 64
    block_row = row_group(place_ref[0])
    block_col = place_ref[0] // 4
    first = block_row == 0
    last = block_row == 3
    odd = block_col % 2 == 1
    right_half = block_col >= 2
    lane = lanes_of((8, 256))
    sub = subs_of((8, 256))
    for k in range(modes_ref.shape[0]):
        here = modes_ref[k, pl.ds(pl.multiple_of(8 * block_row, 8), 8), :]
        before = modes_ref[k, pl.ds(pl.multiple_of(8 * jnp.maximum(block_row - 1, 0), 8), 8), :]
        after = modes_ref[k, pl.ds(pl.multiple_of(8 * jnp.minimum(block_row + 1, 3), 8), 8), :]
        over = jnp.where(first, edge_ref[pl.ds(k, 1), :], before[7:8])
        under = jnp.where(last, edge_ref[pl.ds(k, 1), :], after[0:1])
        up = jnp.where(sub == 0, over, pltpu.roll(here, 1, 0))
        down = jnp.where(sub == 7, under, pltpu.roll(here, 7, 0))
        left = jnp.where(lane == 0, 0.0, pltpu.roll(here, 1, 1))
        right = jnp.where(lane == 255, 0.0, pltpu.roll(here, 255, 1))

        def both(x, y):
            x = 0.5 * (here + x)
            y = 0.5 * (here + y)
            x = jnp.where(right_half, x[:, 128:], x[:, :128])
            y = jnp.where(right_half, y[:, 128:], y[:, :128])
            return jnp.where(
                odd,
                jnp.where(low, pltpu.roll(x, 64, 1), y),
                jnp.where(low, x, pltpu.roll(y, 64, 1)),
            )

        coef_ref[k, pl.ds(0, 8), :] = both(up, down)
        coef_ref[k, pl.ds(8, 8), :] = both(left, right)


def load_kernel(place_ref, index_ref, got_ref, diff_ref):
    lane, sub = lanes_of(), subs_of()
    low = lane < 64
    block_row = row_group(place_ref[0])
    first = block_row == 0
    last = block_row == 3
    over_one = (sub == 0) & jnp.logical_not(first | last)
    over_two = (sub == 0) & last
    under = (sub == 7) & jnp.logical_not(last)
    inner_up = sub > 0
    inner_down = sub < 7

    def load(group, carry):
        tail = got_ref[group, pl.ds(ROWS - 8, 8), :]
        beside = jnp.where(
            sub < 6, pltpu.roll(tail, 6, 0), pltpu.roll(pltpu.roll(tail, 96, 1), 4, 0)
        )
        made = []
        for p in range(PAIRS):
            here = got_ref[group, pl.ds(8 * p, 8), :]
            one = got_ref[group, pl.ds(FIRST + p, 1), :]
            two = got_ref[group, pl.ds(SECOND + p, 1), :]
            above = jnp.where(over_one, one, jnp.where(over_two, two, 0.0))
            below = jnp.where(under, two, 0.0)
            up = here - jnp.where(inner_up, pltpu.roll(here, 1, 0), above)
            down = here - jnp.where(inner_down, pltpu.roll(here, 7, 0), below)
            left = here - jnp.where(
                lane % 64 == 0, pltpu.roll(beside, (128 - 2 * p) % 128, 1), pltpu.roll(here, 1, 1)
            )
            right = here - jnp.where(
                lane % 64 == 63, pltpu.roll(beside, 62 - 2 * p, 1), pltpu.roll(here, 127, 1)
            )
            vert = pltpu.roll(jnp.where(low, down, up), 64, 1)
            hori = pltpu.roll(jnp.where(low, right, left), 64, 1)
            made.append((p, jnp.where(low, up, vert), jnp.where(low, left, hori)))
            made.append((p + PAIRS, jnp.where(low, vert, down), jnp.where(low, hori, right)))
        for i, vert, hori in made:
            term = index_ref[group * (2 * PAIRS) + i]
            diff_ref[term, pl.ds(0, 8), :] = vert
            diff_ref[term, pl.ds(8, 8), :] = hori
        return carry

    lax.fori_loop(0, got_ref.shape[0], load, 0, unroll=4)


def mix_kernel(
    place_ref, index_ref, own_ref, weight_ref, diff_ref, edge_ref, coef_ref, out_ref, diff, total
):
    lane, sub = lanes_of(), subs_of()
    low = lane < 64
    groups = out_ref.shape[0]
    slots = groups * 2 * PAIRS
    first = row_group(place_ref[0]) == 0
    last = row_group(place_ref[0]) == 3
    meets = jnp.where((low & (sub == 0) & first) | ((lane >= 64) & (sub == 7) & last), 1.0, 0.0)

    def own(group, carry):
        edge = edge_ref[pl.ds(pl.multiple_of(8 * group, 8), 8), :]
        more = edge_ref[pl.ds(8 * groups + group, 1), :]
        rows = [edge[p : p + 1] for p in range(8)] + [more]
        coef_v = coef_ref[0, pl.ds(0, 8), :]
        coef_h = coef_ref[0, pl.ds(8, 8), :]
        made = []
        for p in range(PAIRS):
            beyond = jnp.broadcast_to(rows[p], (8, 128))
            turned = pltpu.roll(beyond, 64, 1)
            for o in range(2):
                term = index_ref[group * (2 * PAIRS) + o * PAIRS + p]
                mine = jnp.where(first, beyond, turned) if o == 0 else jnp.where(first, turned, beyond)
                vert = diff_ref[term, pl.ds(0, 8), :] - meets * mine
                hori = diff_ref[term, pl.ds(8, 8), :]
                made.append((term, vert, hori, own_ref[term] * (coef_v * vert + coef_h * hori)))
        for term, vert, hori, value in made:
            diff[term, pl.ds(0, 8), :] = vert
            diff[term, pl.ds(8, 8), :] = hori
            total[term] = value
        return carry

    lax.fori_loop(0, groups, own, 0, unroll=4)

    def couple(step, carry):
        terms = [6 * step + i for i in range(6)]
        uppers, gains, mine = [], [], []
        for term in terms:
            vert = diff[term, pl.ds(0, 8), :]
            hori = diff[term, pl.ds(8, 8), :]
            parts = []
            for v in range(VARS):
                coef_v = coef_ref[v + 1, pl.ds(0, 8), :]
                coef_h = coef_ref[v + 1, pl.ds(8, 8), :]
                upper = index_ref[slots + term * VARS + v]
                uppers.append(upper)
                parts.append(
                    weight_ref[term, pl.ds(v, 1), :]
                    * (coef_v * diff[upper, pl.ds(0, 8), :] + coef_h * diff[upper, pl.ds(8, 8), :])
                )
                gains.append(weight_ref[term, pl.ds(VARS + v, 1), :] * (coef_v * vert + coef_h * hori))
            while len(parts) > 1:
                parts = [x + y for x, y in zip(parts[::2], parts[1::2])] + parts[len(parts) // 2 * 2 :]
            mine.append(parts[0])
        for i, term in enumerate(terms):
            total[term] = total[term] + mine[i]
            sums = [total[uppers[i * VARS + v]] + gains[i * VARS + v] for v in range(VARS)]
            for v in range(VARS):
                total[uppers[i * VARS + v]] = sums[v]
        return carry

    lax.fori_loop(0, LOWER // 6, couple, 0)

    def store(group, carry):
        made = []
        for p in range(PAIRS):
            a = total[index_ref[group * (2 * PAIRS) + p]]
            b = total[index_ref[group * (2 * PAIRS) + PAIRS + p]]
            made.append(jnp.where(low, a, b) + pltpu.roll(jnp.where(low, b, a), 64, 1))
        for p in range(PAIRS):
            out_ref[group, pl.ds(8 * p, 8), :] = made[p]
        return carry

    lax.fori_loop(0, groups, store, 0, unroll=8)


def unpack_kernel(got_ref, out_ref):
    low = lanes_of() < 64
    for r in range(4):
        for h in range(2):
            for p in range(PAIRS):
                one = got_ref[holder(r, 2 * h), pl.ds(8 * p, 8), :]
                two = got_ref[holder(r, 2 * h + 1), pl.ds(8 * p, 8), :]
                out_ref[p, pl.ds(8 * r, 8), pl.ds(128 * h, 128)] = jnp.where(
                    low, one, pltpu.roll(two, 64, 1)
                )
                out_ref[p + PAIRS, pl.ds(8 * r, 8), pl.ds(128 * h, 128)] = jnp.where(
                    low, pltpu.roll(one, 64, 1), two
                )


def vmem():
    return pl.BlockSpec(memory_space=pltpu.VMEM)


def smem():
    return pl.BlockSpec(memory_space=pltpu.SMEM)


def f32(*shape):
    return jax.ShapeDtypeStruct(shape, jnp.float32)


PARAMS = pltpu.CompilerParams(vmem_limit_bytes=32 * 1024 * 1024)


def cost(micros):
    return pl.CostEstimate(flops=0, bytes_accessed=micros * 3000000, transcendentals=0)


def pack(fields, groups):
    return pl.pallas_call(
        pack_kernel,
        out_shape=f32(groups, ROWS, 128),
        in_specs=[vmem()],
        out_specs=vmem(),
        compiler_params=PARAMS,
        cost_estimate=cost(2),
    )(fields)


def edges(got):
    return pl.pallas_call(
        edge_kernel,
        out_shape=f32(got.shape[0] * PAIRS, 128),
        in_specs=[vmem()],
        out_specs=vmem(),
        compiler_params=PARAMS,
        cost_estimate=cost(1),
    )(got)


def coefs(place, modes, edge):
    return pl.pallas_call(
        coef_kernel,
        out_shape=f32(modes.shape[0], 16, 128),
        in_specs=[smem(), vmem(), vmem()],
        out_specs=vmem(),
        compiler_params=PARAMS,
        cost_estimate=cost(1),
    )(place, modes, edge)


def load(place, index, got):
    groups = got.shape[0]
    return pl.pallas_call(
        load_kernel,
        out_shape=f32(groups * 2 * PAIRS, 16, 128),
        in_specs=[smem(), smem(), vmem()],
        out_specs=vmem(),
        compiler_params=PARAMS,
        cost_estimate=cost(4),
    )(place, index, got)


def mix(place, index, own, weights, diff, edge, coef):
    slots = diff.shape[0]
    groups = slots // (2 * PAIRS)
    return pl.pallas_call(
        mix_kernel,
        out_shape=f32(groups, BLOCK, 128),
        in_specs=[smem(), smem(), smem()] + [vmem()] * 4,
        out_specs=vmem(),
        scratch_shapes=[
            pltpu.VMEM((slots, 16, 128), jnp.float32),
            pltpu.VMEM((slots, 8, 128), jnp.float32),
        ],
        compiler_params=PARAMS,
        cost_estimate=cost(5),
    )(place, index, own, weights, diff, edge, coef)


def unpack(got, shape):
    return pl.pallas_call(
        unpack_kernel,
        out_shape=f32(*shape),
        in_specs=[vmem()],
        out_specs=vmem(),
        compiler_params=PARAMS,
        cost_estimate=cost(1),
    )(got)


def tables(pair_list, pair_value, assign):
    terms = assign.shape[0]
    row, col, mode = pair_list[:, 0:1], pair_list[:, 1:2], pair_list[:, 2:3]
    at = jnp.minimum(row, col) == jnp.arange(terms, dtype=jnp.int32)[None, :]
    kinds = jnp.arange(1 + 3 * VARS, dtype=jnp.int32)[None, :]
    wanted = jnp.where(kinds <= VARS, kinds, (kinds - 1) % VARS + 1)
    side = jnp.where(kinds <= VARS, row <= col, jnp.where(kinds <= 2 * VARS, row > col, row < col))
    value = jnp.where(kinds <= 2 * VARS, pair_value[:, None], col.astype(jnp.float32))
    value = jnp.where((mode == wanted) & side, value, 0.0)
    found = lax.dot_general(
        at.astype(jnp.float32),
        value,
        (((0,), (0,)), ((), ())),
        precision=lax.Precision.HIGHEST,
        preferred_element_type=jnp.float32,
    )
    coupled = jnp.pad(found[:LOWER, 1 : 1 + 2 * VARS], ((0, 0), (0, 4)))
    uppers = jnp.round(found[:LOWER, 1 + 2 * VARS :]).astype(jnp.int32).reshape(-1)
    weights = jnp.broadcast_to(coupled[:, :, None], coupled.shape + (128,))
    return jnp.concatenate([assign, uppers]), found[:, 0], weights


def shards(fields, modes, pair_list, pair_value, assign):
    groups = lax.axis_size("term")
    count = lax.axis_size("space")
    passes = []
    for c in range(groups // 4):
        for s in range(count - 1):
            lower, upper = holder(0, c) * count + s + 1, holder(3, c) * count + s
            passes += [(lower, upper), (upper, lower)]
    place = lax.axis_index("term").astype(jnp.int32).reshape(1)
    sent = pack(fields, groups)
    sent, modes = lax.optimization_barrier((sent, modes))
    got = lax.all_to_all(sent, "term", 0, 0, tiled=True)
    index, own, weights = tables(pair_list, pair_value, assign)
    edge = jnp.where(row_group(place[0]) == 0, modes[:, 0], modes[:, modes.shape[1] - 1])
    coef = coefs(place, modes, lax.ppermute(edge, ("term", "space"), passes))
    beyond = lax.ppermute(edges(got), ("term", "space"), passes)
    diff = load(place, index, got)
    mixed = mix(place, index, own, weights, diff, beyond, coef)
    back = lax.all_to_all(mixed, "term", 0, 0, tiled=True)
    return unpack(back, fields.shape)


def solution(mesh):
    return jax.shard_map(
        shards,
        mesh=mesh,
        in_specs=(P("term", "space", None), P(None, "space", None), P(), P(), P()),
        out_specs=P("term", "space", None),
        check_vma=False,
    )
```

time: 83 us -> 69.3 us (0.83)
  Pallas kernels: 15.9 us -> 9.14 us
  blocking collectives: 24.9 us -> 19.8 us
  waiting for transfers between devices: 18 us -> 13.8 us
  matrix products: 1.29 us -> 3.15 us
  starting transfers between devices: 19 us -> 20.8 us
  local copies, waits for them, and re-layouts: 3.11 us -> 2 us
    all_to_all x1, waiting for transfers between devices: 18 us -> 8.62 us  [shards(): got = lax.all_to_all(sent, 'term', 0, 0, tiled=True)]
    pallas_call x2 -> x4, Pallas kernels: 13.1 us -> 6.35 us  [the longest x1 3.78 us: mix(): pl.pallas_call(mix_kernel, out_shape=f32(groups, BLOCK, 128), in_specs=[s...]
    all_to_all x1, blocking collectives: 24.9 us -> 19.8 us  [shards(): back = lax.all_to_all(mixed, 'term', 0, 0, tiled=True)]
    ppermute x2, waiting for transfers between devices: 0.01 us -> 5.15 us  [the longest x1 5.14 us: shards(): beyond = lax.ppermute(edges(got), ('term', 'space'), passes)]
    ppermute x2, starting transfers between devices: 10.4 us -> 12.4 us  [the longest x1 7.73 us: shards(): coef = coefs(place, modes, lax.ppermute(edge, ('term', 'space'), passes))]
    slice x3 -> x2, local copies, waits for them, and re-layouts: 2.01 us -> 0.02 us  [the longest x1 0.02 us: tables(): return (jnp.concatenate([assign, uppers]), found[:, 0], weights)]
    dot_general x1, matrix products: 1.29 us -> 3.15 us  [tables(): lax.dot_general(at.astype(jnp.float32), value, (((0,), (0,)), ((), ())),...]
  transfers between devices with their start and end apart: 3 -> 3, of which waited for: 1 -> 2; matrix products, arithmetic and copies ran while one was open for 2% -> 6% of each run, Pallas kernels for 2% -> 4%
where the time goes in v1:
time: 69.3 us; the launch traced here: 69 us
  starting transfers between devices  20.8 us (30%)
  blocking collectives  19.8 us (29%)
  waiting for transfers between devices  13.8 us (20%)
  Pallas kernels  9.14 us (13%)
  matrix products  3.15 us (5%)
  local copies, waits for them, and re-layouts  2 us (3%)
    all_to_all x1, blocking collectives, shards(): back = lax.all_to_all(mixed, 'term', 0, 0, tiled=True)  19.8 us
    all_to_all x1, waiting for transfers between devices, shards(): got = lax.all_to_all(sent, 'term', 0, 0, tiled=True)  8.62 us
    all_to_all x1, starting transfers between devices, shards(): got = lax.all_to_all(sent, 'term', 0, 0, tiled=True)  8.47 us
    ppermute x1, starting transfers between devices, shards(): coef = coefs(place, modes, lax.ppermute(edge, ('term', 'space'), passes))  7.73 us
    ppermute x1, waiting for transfers between devices, shards(): beyond = lax.ppermute(edges(got), ('term', 'space'), passes)  5.14 us
    ppermute x1, starting transfers between devices, shards(): beyond = lax.ppermute(edges(got), ('term', 'space'), passes)  4.65 us
    pallas_call x1, Pallas kernels, mix(): pl.pallas_call(mix_kernel, out_shape=f32(groups, BLOCK, 128), in_specs=[s...  3.78 us
    dot_general x1, matrix products, tables(): lax.dot_general(at.astype(jnp.float32), value, (((0,), (0,)), ((), ())),...  3.15 us
  transfers between devices with their start and end apart: 3, of which 2 were waited for; matrix products, arithmetic and copies ran while one was open for 6% of the time, Pallas kernels for 4%

profile of v1, /device:TPU:16, one launch (start us, length us, event | category | flops | bytes accessed | tf_op | source)
XLA Modules:
  0.0 69.0 jit_solution(6120090083322900236)
XLA Ops:
  0.0 1.1 %copy-done.1 = f32[18,32,256]{2,1,0:T(8,128)S(1)} copy-done((f32[18,32,256]{2,1,0:T(8,128)S(1)}, f32[18,32,256]{2,1,0:T(8,128)}, u32[]{:S(2)}) %copy-start.1) | copy-done | bytes 589848
  1.1 1.8 %shard_map.55 = f32[16,96,128]{2,1,0:T(8,128)} custom-call(f32[18,32,256]{2,1,0:T(8,128)S(1)} %copy-done.1), custom_call_target="tpu_custom_call" | custom-call | bytes 6000000 | tf_op jit(solution)/shard_map/pallas_call | solution.py:281
  2.9 8.5 %all-to-all-start = ((f32[16,96,128]{2,1,0:T(8,128)}), f32[16,96,128]{2,1,0:T(8,128)S(1)}, u32[]{:S(2)}, u32[]{:S(2)}) async-start(f32[16,96,128]{2,1,0:T(8,128)} %shard_map.55), calls=%async_computation | async-start | bytes 1572864 | tf_op jit(solution)/shard_map/all_to_all | solution.py:386
  11.4 0.0 copy-done
  11.4 0.2 copy.11
  11.6 7.7 %collective-permute-start.1 = (f32[11,256]{1,0:T(8,128)S(1)}, f32[11,256]{1,0:T(8,128)S(1)}, u32[]{:S(2)}, u32[]{:S(2)}) collective-permute-start(f32[11,256]{1,0:T(8,128)S(1)} %fusion.18), channel_id=1, source_target_pairs={{1,48},{48,1},{2,49},{49,2},{3,50},{50,3},{4,51},{51,4},{5,52},{52... | collective-permute-start | bytes 33800 | tf_op jit(solution)/shard_map/ppermute | solution.py:389
  19.4 0.1 compare_reduce_fusion.1
  19.5 0.0 copy-start.3
  19.5 3.2 %fusion = f32[288,31]{0,1:T(8,128)S(1)} fusion(s32[2048]{0:T(1024)S(1)} %bitcast.7, f32[2048]{0:T(1024)S(1)} %bitcast.8, f32[2048]{0:T(1024)S(1)} %copy-done.4, s32[31]{0:T(128)S(1)} %iota_select_fusion, s32[2048]{0:T(1024)S(1)} %bitcast.6, pred[2048]{0:T(1024)(128)(4,1)S(1)} %get-tuple-element.10, pred[31]{0:T(512)(128)(4,1)S(1)} %get-tuple-element.16, ...), kind=kOutput, calls=%fused_computation.1 | convolution fusion | flops 220385280 | bytes 74810 | tf_op jit(solution)/shard_map/dot_general | solution.py:362
  22.7 0.1 copy.9
  22.8 0.1 reshape.44
  23.0 8.6 %all-to-all-done.got_ref = f32[16,96,128]{2,1,0:T(8,128)S(1)} async-done(((f32[16,96,128]{2,1,0:T(8,128)}), f32[16,96,128]{2,1,0:T(8,128)S(1)}, u32[]{:S(2)}, u32[]{:S(2)}) %all-to-all-start) | async-done | bytes 786464 | tf_op jit(solution)/shard_map/all_to_all | solution.py:386
  31.6 4.7 %collective-permute-start = (f32[144,128]{1,0:T(8,128)S(1)}, f32[144,128]{1,0:T(8,128)S(1)}, u32[]{:S(2)}, u32[]{:S(2)}) collective-permute-start(f32[144,128]{1,0:T(8,128)S(1)} %shard_map.57), channel_id=1, source_target_pairs={{1,48},{48,1},{2,49},{49,2},{3,50},{50,3},{4,51},{51,4},{5,52},{52... | collective-permute-start | bytes 221192 | tf_op jit(solution)/shard_map/ppermute | solution.py:390
  36.3 0.0 copy-done.3
  36.3 0.1 pad_add_fusion.index_ref
  36.4 0.1 copy.13
  36.5 0.0 collective-permute-done.1.edge_ref
  36.5 0.2 shard_map.58.coef_ref
  36.7 2.4 %shard_map.56.diff_ref = f32[288,16,128]{2,1,0:T(8,128)S(1)} custom-call(s32[1]{0:T(128)} %bitcast.place_ref, s32[948]{0:T(1024)S(1)} %pad_add_fusion.index_ref, f32[16,96,128]{2,1,0:T(8,128)S(1)} %all-to-all-done.got_ref), custom_call_target="tpu_custom_call" | custom-call | bytes 12000000 | tf_op jit(solution)/shard_map/pallas_call | solution.py:315
  39.1 5.1 %collective-permute-done.edge_ref = f32[144,128]{1,0:T(8,128)S(1)} collective-permute-done((f32[144,128]{1,0:T(8,128)S(1)}, f32[144,128]{1,0:T(8,128)S(1)}, u32[]{:S(2)}, u32[]{:S(2)}) %collective-permute-start) | collective-permute-done | bytes 73760 | tf_op jit(solution)/shard_map/ppermute | solution.py:390
  44.2 0.3 broadcast_in_dim.97.weight_ref
  44.5 3.8 %shard_map.59 = f32[16,72,128]{2,1,0:T(8,128)S(1)} custom-call(s32[1]{0:T(128)} %bitcast.place_ref, s32[948]{0:T(1024)S(1)} %pad_add_fusion.index_ref, f32[288]{0:T(512)S(1)} %slice_reduce_fusion.own_ref, f32[66,24,128]{2,1,0:T(8,128)S(1)} %broadcast_in_dim.97.weight_ref, f32[288,16,128]{2,1,0:T(8,128)S(1)} %shard_map.56.diff_ref, ...), custom_call_target="tpu_custom_call" | custom-call | bytes 15000000 | tf_op jit(solution)/shard_map/pallas_call | solution.py:328
  48.2 19.8 %all_to_all.10.got_ref = f32[16,72,128]{2,1,0:T(8,128)S(1)} all-to-all(f32[16,72,128]{2,1,0:T(8,128)S(1)} %shard_map.59), channel_id=1, replica_groups=mesh['term'=16,'space'=16] {'term'}, dimensions={0} | all-to-all | bytes 1179648 | tf_op jit(solution)/shard_map/all_to_all | solution.py:393
  68.0 1.0 %shard_map.60 = f32[18,32,256]{2,1,0:T(8,128)} custom-call(f32[16,72,128]{2,1,0:T(8,128)S(1)} %all_to_all.10.got_ref), custom_call_target="tpu_custom_call" | custom-call | bytes 3000000 | tf_op jit(solution)/shard_map/pallas_call | solution.py:343
  (15 shorter events, 0.1 us)
Async XLA Ops:
  0.0 11.4 %copy-start = (f32[11,32,256]{2,1,0:T(8,128)S(1)}, f32[11,32,256]{2,1,0:T(8,128)}, u32[]{:S(2)}) copy-start(f32[11,32,256]{2,1,0:T(8,128)} %modes_ref) | copy-start | bytes 1081348
  0.0 1.1 %copy-start.1 = (f32[18,32,256]{2,1,0:T(8,128)S(1)}, f32[18,32,256]{2,1,0:T(8,128)}, u32[]{:S(2)}) copy-start(f32[18,32,256]{2,1,0:T(8,128)} %f_ref.1) | copy-start | bytes 1769476
  1.1 18.3 %copy-start.2 = (s32[2048,3]{0,1:T(4,128)S(1)}, s32[2048,3]{0,1:T(4,128)}, u32[]{:S(2)}) copy-start(s32[2048,3]{0,1:T(4,128)} %param.7) | copy-start | bytes 73732
  1.1 18.4 %copy-start.4 = (f32[2048]{0:T(1024)S(1)}, f32[2048]{0:T(1024)}, u32[]{:S(2)}) copy-start(f32[2048]{0:T(1024)} %param.8) | copy-start | bytes 24580
  2.9 28.7 %all-to-all-start = ((f32[16,96,128]{2,1,0:T(8,128)}), f32[16,96,128]{2,1,0:T(8,128)S(1)}, u32[]{:S(2)}, u32[]{:S(2)}) async-start(f32[16,96,128]{2,1,0:T(8,128)} %shard_map.55), calls=%async_computation | async-start | bytes 1572864 | tf_op jit(solution)/shard_map/all_to_all | solution.py:386
  11.6 24.9 %collective-permute-start.1 = (f32[11,256]{1,0:T(8,128)S(1)}, f32[11,256]{1,0:T(8,128)S(1)}, u32[]{:S(2)}, u32[]{:S(2)}) collective-permute-start(f32[11,256]{1,0:T(8,128)S(1)} %fusion.18), channel_id=1, source_target_pairs={{1,48},{48,1},{2,49},{49,2},{3,50},{50,3},{4,51},{51,4},{5,52},{52... | collective-permute-start | bytes 33800 | tf_op jit(solution)/shard_map/ppermute | solution.py:389
  19.5 16.8 %copy-start.3 = (s32[288]{0:T(512)S(1)}, s32[288]{0:T(512)}, u32[]{:S(2)}) copy-start(s32[288]{0:T(512)} %param.9) | copy-start | bytes 3460
  31.6 12.6 %collective-permute-start = (f32[144,128]{1,0:T(8,128)S(1)}, f32[144,128]{1,0:T(8,128)S(1)}, u32[]{:S(2)}, u32[]{:S(2)}) collective-permute-start(f32[144,128]{1,0:T(8,128)S(1)} %shard_map.57), channel_id=1, source_target_pairs={{1,48},{48,1},{2,49},{49,2},{3,50},{50,3},{4,51},{51,4},{5,52},{52... | collective-permute-start | bytes 221192 | tf_op jit(solution)/shard_map/ppermute | solution.py:390

commit v2 on v1

--- a/solution.py
+++ b/solution.py
@@ -19,6 +19,15 @@
     return 4 * c + (r ^ c)
 
 
+def mask_at(space):
+    return (space >> 1 & 1) * 8 + (space & 1) * 3
+
+
+def here():
+    mask = mask_at(lax.axis_index("space"))
+    return mask, lax.axis_index("term") ^ mask
+
+
 def row_group(place):
     return (place & 3) ^ (place >> 2)
 
@@ -36,6 +45,7 @@
     low = lane < 64
     even = lane % 2 == 0
     spare = lane % 64 >= 32
+    mask, _ = here()
     for r in range(4):
         near, far = [], []
         for h in range(2):
@@ -51,18 +61,18 @@
                 for o in range(2):
                     c = 2 * h + o
                     first, last = both[o][0:1], both[o][7:8]
-                    out_ref[holder(r, c), pl.ds(8 * p, 8), :] = both[o]
+                    out_ref[holder(r, c) ^ mask, pl.ds(8 * p, 8), :] = both[o]
                     if r == 0:
-                        out_ref[holder(0, c), pl.ds(FIRST + p, 1), :] = first
+                        out_ref[holder(0, c) ^ mask, pl.ds(FIRST + p, 1), :] = first
                     if r == 3:
-                        out_ref[holder(3, c), pl.ds(FIRST + p, 1), :] = last
+                        out_ref[holder(3, c) ^ mask, pl.ds(FIRST + p, 1), :] = last
                     if r < 3:
-                        out_ref[holder(r + 1, c), pl.ds((FIRST if r < 2 else SECOND) + p, 1), :] = last
+                        out_ref[holder(r + 1, c) ^ mask, pl.ds((FIRST if r < 2 else SECOND) + p, 1), :] = last
                     if r > 0:
-                        out_ref[holder(r - 1, c), pl.ds(SECOND + p, 1), :] = first
-                here = (lane % 64) // 2 == p
-                ga = jnp.where(here, pltpu.roll(a, (2 * p - 63) % 128, 1), ga)
-                gb = jnp.where(here, pltpu.roll(b, 2 * p + 1, 1), gb)
+                        out_ref[holder(r - 1, c) ^ mask, pl.ds(SECOND + p, 1), :] = first
+                pair = (lane % 64) // 2 == p
+                ga = jnp.where(pair, pltpu.roll(a, (2 * p - 63) % 128, 1), ga)
+                gb = jnp.where(pair, pltpu.roll(b, 2 * p + 1, 1), gb)
             near.append(jnp.where(low, ga, gb))
             far.append(pltpu.roll(jnp.where(low, gb, ga), 64, 1))
         zero = jnp.zeros((8, 128), jnp.float32)
@@ -75,7 +85,7 @@
         for c in range(4):
             moved = pltpu.roll(pltpu.roll(sides[c], 32, 1), 2, 0)
             kept = jnp.where(spare, moved, sides[c])
-            out_ref[holder(r, c), pl.ds(SIDE, 6), :] = kept[0:6]
+            out_ref[holder(r, c) ^ mask, pl.ds(SIDE, 6), :] = kept[0:6]
 
 
 def edge_kernel(got_ref, edge_ref):
@@ -85,10 +95,11 @@
         edge_ref[pl.ds(8 * groups + group, 1), :] = got_ref[group, pl.ds(FIRST + 8, 1), :]
 
 
-def coef_kernel(place_ref, modes_ref, edge_ref, coef_ref):
+def coef_kernel(modes_ref, edge_ref, weight_ref, coef_ref):
+    _, place = here()
     low = lanes_of() < 64
-    block_row = row_group(place_ref[0])
-    block_col = place_ref[0] // 4
+    block_row = row_group(place)
+    block_col = place >> 2
     first = block_row == 0
     last = block_row == 3
     odd = block_col % 2 == 1
@@ -96,19 +107,19 @@
     lane = lanes_of((8, 256))
     sub = subs_of((8, 256))
     for k in range(modes_ref.shape[0]):
-        here = modes_ref[k, pl.ds(pl.multiple_of(8 * block_row, 8), 8), :]
+        cells = modes_ref[k, pl.ds(pl.multiple_of(8 * block_row, 8), 8), :]
         before = modes_ref[k, pl.ds(pl.multiple_of(8 * jnp.maximum(block_row - 1, 0), 8), 8), :]
         after = modes_ref[k, pl.ds(pl.multiple_of(8 * jnp.minimum(block_row + 1, 3), 8), 8), :]
         over = jnp.where(first, edge_ref[pl.ds(k, 1), :], before[7:8])
         under = jnp.where(last, edge_ref[pl.ds(k, 1), :], after[0:1])
-        up = jnp.where(sub == 0, over, pltpu.roll(here, 1, 0))
-        down = jnp.where(sub == 7, under, pltpu.roll(here, 7, 0))
-        left = jnp.where(lane == 0, 0.0, pltpu.roll(here, 1, 1))
-        right = jnp.where(lane == 255, 0.0, pltpu.roll(here, 255, 1))
+        up = jnp.where(sub == 0, over, pltpu.roll(cells, 1, 0))
+        down = jnp.where(sub == 7, under, pltpu.roll(cells, 7, 0))
+        left = jnp.where(lane == 0, 0.0, pltpu.roll(cells, 1, 1))
+        right = jnp.where(lane == 255, 0.0, pltpu.roll(cells, 255, 1))
 
         def both(x, y):
-            x = 0.5 * (here + x)
-            y = 0.5 * (here + y)
+            x = 0.5 * (cells + x)
+            y = 0.5 * (cells + y)
             x = jnp.where(right_half, x[:, 128:], x[:, :128])
             y = jnp.where(right_half, y[:, 128:], y[:, :128])
             return jnp.where(
@@ -121,10 +132,11 @@
         coef_ref[k, pl.ds(8, 8), :] = both(left, right)
 
 
-def load_kernel(place_ref, index_ref, got_ref, diff_ref):
+def load_kernel(index_ref, got_ref, diff_ref):
+    _, place = here()
     lane, sub = lanes_of(), subs_of()
     low = lane < 64
-    block_row = row_group(place_ref[0])
+    block_row = row_group(place)
     first = block_row == 0
     last = block_row == 3
     over_one = (sub == 0) & jnp.logical_not(first | last)
@@ -140,18 +152,18 @@
         )
         made = []
         for p in range(PAIRS):
-            here = got_ref[group, pl.ds(8 * p, 8), :]
+            cells = got_ref[group, pl.ds(8 * p, 8), :]
             one = got_ref[group, pl.ds(FIRST + p, 1), :]
             two = got_ref[group, pl.ds(SECOND + p, 1), :]
             above = jnp.where(over_one, one, jnp.where(over_two, two, 0.0))
             below = jnp.where(under, two, 0.0)
-            up = here - jnp.where(inner_up, pltpu.roll(here, 1, 0), above)
-            down = here - jnp.where(inner_down, pltpu.roll(here, 7, 0), below)
-            left = here - jnp.where(
-                lane % 64 == 0, pltpu.roll(beside, (128 - 2 * p) % 128, 1), pltpu.roll(here, 1, 1)
+            up = cells - jnp.where(inner_up, pltpu.roll(cells, 1, 0), above)
+            down = cells - jnp.where(inner_down, pltpu.roll(cells, 7, 0), below)
+            left = cells - jnp.where(
+                lane % 64 == 0, pltpu.roll(beside, (128 - 2 * p) % 128, 1), pltpu.roll(cells, 1, 1)
             )
-            right = here - jnp.where(
-                lane % 64 == 63, pltpu.roll(beside, 62 - 2 * p, 1), pltpu.roll(here, 127, 1)
+            right = cells - jnp.where(
+                lane % 64 == 63, pltpu.roll(beside, 62 - 2 * p, 1), pltpu.roll(cells, 127, 1)
             )
             vert = pltpu.roll(jnp.where(low, down, up), 64, 1)
             hori = pltpu.roll(jnp.where(low, right, left), 64, 1)
@@ -167,14 +179,15 @@
 
 
 def mix_kernel(
-    place_ref, index_ref, own_ref, weight_ref, diff_ref, edge_ref, coef_ref, out_ref, diff, total
+    index_ref, own_ref, weight_ref, diff_ref, edge_ref, coef_ref, out_ref, diff, total
 ):
+    _, place = here()
     lane, sub = lanes_of(), subs_of()
     low = lane < 64
     groups = out_ref.shape[0]
     slots = groups * 2 * PAIRS
-    first = row_group(place_ref[0]) == 0
-    last = row_group(place_ref[0]) == 3
+    first = row_group(place) == 0
+    last = row_group(place) == 3
     meets = jnp.where((low & (sub == 0) & first) | ((lane >= 64) & (sub == 7) & last), 1.0, 0.0)
 
     def own(group, carry):
@@ -245,11 +258,12 @@
 
 def unpack_kernel(got_ref, out_ref):
     low = lanes_of() < 64
+    mask, _ = here()
     for r in range(4):
         for h in range(2):
             for p in range(PAIRS):
-                one = got_ref[holder(r, 2 * h), pl.ds(8 * p, 8), :]
-                two = got_ref[holder(r, 2 * h + 1), pl.ds(8 * p, 8), :]
+                one = got_ref[holder(r, 2 * h) ^ mask, pl.ds(8 * p, 8), :]
+                two = got_ref[holder(r, 2 * h + 1) ^ mask, pl.ds(8 * p, 8), :]
                 out_ref[p, pl.ds(8 * r, 8), pl.ds(128 * h, 128)] = jnp.where(
                     low, one, pltpu.roll(two, 64, 1)
                 )
@@ -299,36 +313,36 @@
     )(got)
 
 
-def coefs(place, modes, edge):
+def coefs(modes, edge, weights):
     return pl.pallas_call(
         coef_kernel,
         out_shape=f32(modes.shape[0], 16, 128),
-        in_specs=[smem(), vmem(), vmem()],
+        in_specs=[vmem(), vmem(), pl.BlockSpec(memory_space=pl.ANY)],
         out_specs=vmem(),
         compiler_params=PARAMS,
         cost_estimate=cost(1),
-    )(place, modes, edge)
-
-
-def load(place, index, got):
+    )(modes, edge, weights)
+
+
+def load(index, got):
     groups = got.shape[0]
     return pl.pallas_call(
         load_kernel,
         out_shape=f32(groups * 2 * PAIRS, 16, 128),
-        in_specs=[smem(), smem(), vmem()],
+        in_specs=[smem(), vmem()],
         out_specs=vmem(),
         compiler_params=PARAMS,
         cost_estimate=cost(4),
-    )(place, index, got)
-
-
-def mix(place, index, own, weights, diff, edge, coef):
+    )(index, got)
+
+
+def mix(index, own, weights, diff, edge, coef):
     slots = diff.shape[0]
     groups = slots // (2 * PAIRS)
     return pl.pallas_call(
         mix_kernel,
         out_shape=f32(groups, BLOCK, 128),
-        in_specs=[smem(), smem(), smem()] + [vmem()] * 4,
+        in_specs=[smem(), smem()] + [vmem()] * 4,
         out_specs=vmem(),
         scratch_shapes=[
             pltpu.VMEM((slots, 16, 128), jnp.float32),
@@ -336,7 +350,7 @@
         ],
         compiler_params=PARAMS,
         cost_estimate=cost(5),
-    )(place, index, own, weights, diff, edge, coef)
+    )(index, own, weights, diff, edge, coef)
 
 
 def unpack(got, shape):
@@ -378,18 +392,20 @@
     passes = []
     for c in range(groups // 4):
         for s in range(count - 1):
-            lower, upper = holder(0, c) * count + s + 1, holder(3, c) * count + s
+            lower = (holder(0, c) ^ mask_at(s + 1)) * count + s + 1
+            upper = (holder(3, c) ^ mask_at(s)) * count + s
             passes += [(lower, upper), (upper, lower)]
-    place = lax.axis_index("term").astype(jnp.int32).reshape(1)
     sent = pack(fields, groups)
     sent, modes = lax.optimization_barrier((sent, modes))
     got = lax.all_to_all(sent, "term", 0, 0, tiled=True)
     index, own, weights = tables(pair_list, pair_value, assign)
-    edge = jnp.where(row_group(place[0]) == 0, modes[:, 0], modes[:, modes.shape[1] - 1])
-    coef = coefs(place, modes, lax.ppermute(edge, ("term", "space"), passes))
+    _, place = here()
+    edge = jnp.where(row_group(place) == 0, modes[:, 0], modes[:, modes.shape[1] - 1])
+    coef = coefs(modes, lax.ppermute(edge, ("term", "space"), passes), weights)
+    got, coef, index = lax.optimization_barrier((got, coef, index))
     beyond = lax.ppermute(edges(got), ("term", "space"), passes)
-    diff = load(place, index, got)
-    mixed = mix(place, index, own, weights, diff, beyond, coef)
+    diff = load(index, got)
+    mixed = mix(index, own, weights, diff, beyond, coef)
     back = lax.all_to_all(mixed, "term", 0, 0, tiled=True)
     return unpack(back, fields.shape)
 

time: 69.3 us -> 67.8 us (0.978)
  waiting for transfers between devices: 13.8 us -> 11.1 us
  blocking collectives: 19.8 us -> 22.3 us
  starting transfers between devices: 20.8 us -> 19.6 us
    ppermute x1, waiting for transfers between devices: 5.14 us -> 1.17 us  [shards(): beyond = lax.ppermute(edges(got), ('term', 'space'), passes)]
    all_to_all x1, blocking collectives: 19.8 us -> 22.3 us  [shards(): back = lax.all_to_all(mixed, 'term', 0, 0, tiled=True)]
    ppermute x1, starting transfers between devices: 7.73 us -> 5.62 us  [shards(): coef = coefs(modes, lax.ppermute(edge, ('term', 'space'), passes), weights)]
    all_to_all x1, waiting for transfers between devices: 8.62 us -> 9.94 us  [shards(): got = lax.all_to_all(sent, 'term', 0, 0, tiled=True)]
    ppermute x1, starting transfers between devices: 4.65 us -> 5.53 us  [shards(): beyond = lax.ppermute(edges(got), ('term', 'space'), passes)]
where the time goes in v2:
time: 67.8 us; the launch traced here: 67.6 us
  blocking collectives  22.3 us (33%)
  starting transfers between devices  19.6 us (29%)
  waiting for transfers between devices  11.1 us (16%)
  Pallas kernels  8.98 us (13%)
  matrix products  3.15 us (5%)
  local copies, waits for them, and re-layouts  2 us (3%)
    all_to_all x1, blocking collectives, shards(): back = lax.all_to_all(mixed, 'term', 0, 0, tiled=True)  22.3 us
    all_to_all x1, waiting for transfers between devices, shards(): got = lax.all_to_all(sent, 'term', 0, 0, tiled=True)  9.94 us
    all_to_all x1, starting transfers between devices, shards(): got = lax.all_to_all(sent, 'term', 0, 0, tiled=True)  8.47 us
    ppermute x1, starting transfers between devices, shards(): coef = coefs(modes, lax.ppermute(edge, ('term', 'space'), passes), weights)  5.62 us
    ppermute x1, starting transfers between devices, shards(): beyond = lax.ppermute(edges(got), ('term', 'space'), passes)  5.53 us
    pallas_call x1, Pallas kernels, mix(): pl.pallas_call(mix_kernel, out_shape=f32(groups, BLOCK, 128), in_specs=[s...  3.75 us
    dot_general x1, matrix products, tables(): lax.dot_general(at.astype(jnp.float32), value, (((0,), (0,)), ((), ())),...  3.15 us
    pallas_call x1, Pallas kernels, load(): pl.pallas_call(load_kernel, out_shape=f32(groups * 2 * PAIRS, 16, 128), i...  2.38 us
  transfers between devices with their start and end apart: 3, of which 2 were waited for; matrix products, arithmetic and copies ran while one was open for 6% of the time, Pallas kernels for 4%

profile of v2, /device:TPU:16, one launch (start us, length us, event | category | flops | bytes accessed | tf_op | source)
XLA Modules:
  0.0 67.6 jit_solution(2867374934285439885)
XLA Ops:
  0.0 1.1 %copy-done.1 = f32[18,32,256]{2,1,0:T(8,128)S(1)} copy-done((f32[18,32,256]{2,1,0:T(8,128)S(1)}, f32[18,32,256]{2,1,0:T(8,128)}, u32[]{:S(2)}) %copy-start.1) | copy-done | bytes 589848
  1.1 1.6 %shard_map.55 = f32[16,96,128]{2,1,0:T(8,128)} custom-call(f32[18,32,256]{2,1,0:T(8,128)S(1)} %copy-done.1), custom_call_target="tpu_custom_call" | custom-call | bytes 6000000 | tf_op jit(solution)/shard_map/pallas_call | solution.py:295
  2.7 8.5 %all-to-all-start = ((f32[16,96,128]{2,1,0:T(8,128)}), f32[16,96,128]{2,1,0:T(8,128)S(1)}, u32[]{:S(2)}, u32[]{:S(2)}) async-start(f32[16,96,128]{2,1,0:T(8,128)} %shard_map.55), calls=%async_computation | async-start | bytes 1572864 | tf_op jit(solution)/shard_map/all_to_all | solution.py:400
  11.2 0.0 copy-done
  11.2 0.0 copy-start.3
  11.2 0.2 copy.9
  11.5 5.6 %collective-permute-start = (f32[11,256]{1,0:T(8,128)S(1)}, f32[11,256]{1,0:T(8,128)S(1)}, u32[]{:S(2)}, u32[]{:S(2)}) collective-permute-start(f32[11,256]{1,0:T(8,128)S(1)} %fusion.18), channel_id=1, source_target_pairs={{49,48},{48,49},{130,1},{1,130},{179,178},{178,179},{4,131},{131,4... | collective-permute-start | bytes 33800 | tf_op jit(solution)/shard_map/ppermute | solution.py:404
  17.1 0.0 copy-done.2
  17.1 0.1 compare_reduce_fusion.1
  17.3 3.2 %fusion = f32[288,31]{0,1:T(8,128)S(1)} fusion(s32[2048]{0:T(1024)S(1)} %bitcast.6, f32[2048]{0:T(1024)S(1)} %bitcast.7, f32[2048]{0:T(1024)S(1)} %copy-done.4, s32[31]{0:T(128)S(1)} %iota_select_fusion, s32[2048]{0:T(1024)S(1)} %bitcast.5, pred[2048]{0:T(1024)(128)(4,1)S(1)} %get-tuple-element.16, pred[31]{0:T(512)(128)(4,1)S(1)} %get-tuple-element.22, ...), kind=kOutput, calls=%fused_computation.1 | convolution fusion | flops 220385280 | bytes 74810 | tf_op jit(solution)/shard_map/dot_general | solution.py:376
  20.4 0.1 copy.12
  20.5 0.1 reshape.40
  20.7 0.1 pad_add_fusion.index_ref
  20.8 0.1 copy.13
  20.9 0.0 collective-permute-done.edge_ref
  20.9 0.3 broadcast_in_dim.97.weight_ref
  21.2 0.2 shard_map.56.coef_ref
  21.4 9.9 %all-to-all-done.got_ref = f32[16,96,128]{2,1,0:T(8,128)S(1)} async-done(((f32[16,96,128]{2,1,0:T(8,128)}), f32[16,96,128]{2,1,0:T(8,128)S(1)}, u32[]{:S(2)}, u32[]{:S(2)}) %all-to-all-start) | async-done | bytes 786464 | tf_op jit(solution)/shard_map/all_to_all | solution.py:400
  31.3 5.5 %collective-permute-start.1 = (f32[144,128]{1,0:T(8,128)S(1)}, f32[144,128]{1,0:T(8,128)S(1)}, u32[]{:S(2)}, u32[]{:S(2)}) collective-permute-start(f32[144,128]{1,0:T(8,128)S(1)} %shard_map.58), channel_id=1, source_target_pairs={{49,48},{48,49},{130,1},{1,130},{179,178},{178,179},{4,131},{131,4... | collective-permute-start | bytes 221192 | tf_op jit(solution)/shard_map/ppermute | solution.py:406
  36.9 2.4 %shard_map.57.diff_ref = f32[288,16,128]{2,1,0:T(8,128)S(1)} custom-call(s32[948]{0:T(1024)S(1)} %pad_add_fusion.index_ref, f32[16,96,128]{2,1,0:T(8,128)S(1)} %all-to-all-done.got_ref), custom_call_target="tpu_custom_call" | custom-call | bytes 12000000 | tf_op jit(solution)/shard_map/pallas_call | solution.py:329
  39.3 1.2 %collective-permute-done.1.edge_ref = f32[144,128]{1,0:T(8,128)S(1)} collective-permute-done((f32[144,128]{1,0:T(8,128)S(1)}, f32[144,128]{1,0:T(8,128)S(1)}, u32[]{:S(2)}, u32[]{:S(2)}) %collective-permute-start.1) | collective-permute-done | bytes 73760 | tf_op jit(solution)/shard_map/ppermute | solution.py:406
  40.4 3.7 %shard_map.59 = f32[16,72,128]{2,1,0:T(8,128)S(1)} custom-call(s32[948]{0:T(1024)S(1)} %pad_add_fusion.index_ref, f32[288]{0:T(512)S(1)} %slice_reduce_fusion.own_ref, f32[66,24,128]{2,1,0:T(8,128)S(1)} %broadcast_in_dim.97.weight_ref, f32[288,16,128]{2,1,0:T(8,128)S(1)} %shard_map.57.diff_ref, f32[144,128]{1,0:T(8,128)S(1)} %collective-permute-done.1.edge_ref, ...), custom_call_target="tpu_custom_call" | custom-call | bytes 15000000 | tf_op jit(solution)/shard_map/pallas_call | solution.py:342
  44.2 22.3 %all_to_all.10.got_ref = f32[16,72,128]{2,1,0:T(8,128)S(1)} all-to-all(f32[16,72,128]{2,1,0:T(8,128)S(1)} %shard_map.59), channel_id=1, replica_groups=mesh['term'=16,'space'=16] {'term'}, dimensions={0} | all-to-all | bytes 1179648 | tf_op jit(solution)/shard_map/all_to_all | solution.py:409
  66.5 1.0 %shard_map.60 = f32[18,32,256]{2,1,0:T(8,128)} custom-call(f32[16,72,128]{2,1,0:T(8,128)S(1)} %all_to_all.10.got_ref), custom_call_target="tpu_custom_call" | custom-call | bytes 3000000 | tf_op jit(solution)/shard_map/pallas_call | solution.py:357
  (15 shorter events, 0.1 us)
Async XLA Ops:
  0.0 11.2 %copy-start = (f32[11,32,256]{2,1,0:T(8,128)S(1)}, f32[11,32,256]{2,1,0:T(8,128)}, u32[]{:S(2)}) copy-start(f32[11,32,256]{2,1,0:T(8,128)} %modes_ref) | copy-start | bytes 1081348
  0.0 1.1 %copy-start.1 = (f32[18,32,256]{2,1,0:T(8,128)S(1)}, f32[18,32,256]{2,1,0:T(8,128)}, u32[]{:S(2)}) copy-start(f32[18,32,256]{2,1,0:T(8,128)} %f_ref.1) | copy-start | bytes 1769476
  1.1 16.0 %copy-start.2 = (s32[2048,3]{0,1:T(4,128)S(1)}, s32[2048,3]{0,1:T(4,128)}, u32[]{:S(2)}) copy-start(s32[2048,3]{0,1:T(4,128)} %param.7) | copy-start | bytes 73732
  1.1 16.1 %copy-start.4 = (f32[2048]{0:T(1024)S(1)}, f32[2048]{0:T(1024)}, u32[]{:S(2)}) copy-start(f32[2048]{0:T(1024)} %param.8) | copy-start | bytes 24580
  2.7 28.6 %all-to-all-start = ((f32[16,96,128]{2,1,0:T(8,128)}), f32[16,96,128]{2,1,0:T(8,128)S(1)}, u32[]{:S(2)}, u32[]{:S(2)}) async-start(f32[16,96,128]{2,1,0:T(8,128)} %shard_map.55), calls=%async_computation | async-start | bytes 1572864 | tf_op jit(solution)/shard_map/all_to_all | solution.py:400
  11.2 9.5 %copy-start.3 = (s32[288]{0:T(512)S(1)}, s32[288]{0:T(512)}, u32[]{:S(2)}) copy-start(s32[288]{0:T(512)} %param.9) | copy-start | bytes 3460
  11.5 9.4 %collective-permute-start = (f32[11,256]{1,0:T(8,128)S(1)}, f32[11,256]{1,0:T(8,128)S(1)}, u32[]{:S(2)}, u32[]{:S(2)}) collective-permute-start(f32[11,256]{1,0:T(8,128)S(1)} %fusion.18), channel_id=1, source_target_pairs={{49,48},{48,49},{130,1},{1,130},{179,178},{178,179},{4,131},{131,4... | collective-permute-start | bytes 33800 | tf_op jit(solution)/shard_map/ppermute | solution.py:404
  31.3 9.1 %collective-permute-start.1 = (f32[144,128]{1,0:T(8,128)S(1)}, f32[144,128]{1,0:T(8,128)S(1)}, u32[]{:S(2)}, u32[]{:S(2)}) collective-permute-start(f32[144,128]{1,0:T(8,128)S(1)} %shard_map.58), channel_id=1, source_target_pairs={{49,48},{48,49},{130,1},{1,130},{179,178},{178,179},{4,131},{131,4... | collective-permute-start | bytes 221192 | tf_op jit(solution)/shard_map/ppermute | solution.py:406

commit v3 on v2

--- a/solution.py
+++ b/solution.py
@@ -40,12 +40,17 @@
     return lax.broadcasted_iota(jnp.int32, shape, 0)
 
 
-def pack_kernel(f_ref, out_ref):
+def pack_kernel(f_ref, sent_ref, out_ref, out_sem):
     lane = lanes_of()
     low = lane < 64
     even = lane % 2 == 0
     spare = lane % 64 >= 32
     mask, _ = here()
+
+    def send(r, c):
+        to = holder(r, c) ^ mask
+        return pltpu.make_async_copy(out_ref.at[to], sent_ref.at[to], out_sem.at[4 * r + c])
+
     for r in range(4):
         near, far = [], []
         for h in range(2):
@@ -86,6 +91,13 @@
             moved = pltpu.roll(pltpu.roll(sides[c], 32, 1), 2, 0)
             kept = jnp.where(spare, moved, sides[c])
             out_ref[holder(r, c) ^ mask, pl.ds(SIDE, 6), :] = kept[0:6]
+        for done in ((r - 1, r) if r == 3 else (r - 1,)):
+            if done >= 0:
+                for c in range(4):
+                    send(done, c).start()
+    for r in range(4):
+        for c in range(4):
+            send(r, c).wait()
 
 
 def edge_kernel(got_ref, edge_ref):
@@ -132,7 +144,7 @@
         coef_ref[k, pl.ds(8, 8), :] = both(left, right)
 
 
-def load_kernel(index_ref, got_ref, diff_ref):
+def load_kernel(own_ref, got_ref, coef_ref, diff_ref, total_ref):
     _, place = here()
     lane, sub = lanes_of(), subs_of()
     low = lane < 64
@@ -169,62 +181,68 @@
             hori = pltpu.roll(jnp.where(low, right, left), 64, 1)
             made.append((p, jnp.where(low, up, vert), jnp.where(low, left, hori)))
             made.append((p + PAIRS, jnp.where(low, vert, down), jnp.where(low, hori, right)))
+        coef_v = coef_ref[0, pl.ds(0, 8), :]
+        coef_h = coef_ref[0, pl.ds(8, 8), :]
         for i, vert, hori in made:
-            term = index_ref[group * (2 * PAIRS) + i]
-            diff_ref[term, pl.ds(0, 8), :] = vert
-            diff_ref[term, pl.ds(8, 8), :] = hori
+            slot = group * (2 * PAIRS) + i
+            diff_ref[slot, pl.ds(0, 8), :] = vert
+            diff_ref[slot, pl.ds(8, 8), :] = hori
+            total_ref[slot] = own_ref[pl.ds(slot, 1), :] * (coef_v * vert + coef_h * hori)
         return carry
 
-    lax.fori_loop(0, got_ref.shape[0], load, 0, unroll=4)
+    lax.fori_loop(0, got_ref.shape[0], load, 0, unroll=2)
 
 
 def mix_kernel(
-    index_ref, own_ref, weight_ref, diff_ref, edge_ref, coef_ref, out_ref, diff, total
+    place_ref, own_ref, weight_ref, diff_ref, start_ref, edge_ref, coef_ref, out_ref, diff, total, places, sem
 ):
+    copy = pltpu.make_async_copy(place_ref, places, sem)
+    copy.start()
     _, place = here()
     lane, sub = lanes_of(), subs_of()
     low = lane < 64
     groups = out_ref.shape[0]
-    slots = groups * 2 * PAIRS
     first = row_group(place) == 0
     last = row_group(place) == 3
     meets = jnp.where((low & (sub == 0) & first) | ((lane >= 64) & (sub == 7) & last), 1.0, 0.0)
 
-    def own(group, carry):
+    def patch(group, carry):
         edge = edge_ref[pl.ds(pl.multiple_of(8 * group, 8), 8), :]
         more = edge_ref[pl.ds(8 * groups + group, 1), :]
-        rows = [edge[p : p + 1] for p in range(8)] + [more]
+        rows = []
+        for part in (edge, more):
+            turned = pltpu.roll(part, 64, 1)
+            rows.append((jnp.where(first, part, turned), jnp.where(first, turned, part)))
         coef_v = coef_ref[0, pl.ds(0, 8), :]
-        coef_h = coef_ref[0, pl.ds(8, 8), :]
         made = []
         for p in range(PAIRS):
-            beyond = jnp.broadcast_to(rows[p], (8, 128))
-            turned = pltpu.roll(beyond, 64, 1)
             for o in range(2):
-                term = index_ref[group * (2 * PAIRS) + o * PAIRS + p]
-                mine = jnp.where(first, beyond, turned) if o == 0 else jnp.where(first, turned, beyond)
-                vert = diff_ref[term, pl.ds(0, 8), :] - meets * mine
-                hori = diff_ref[term, pl.ds(8, 8), :]
-                made.append((term, vert, hori, own_ref[term] * (coef_v * vert + coef_h * hori)))
-        for term, vert, hori, value in made:
-            diff[term, pl.ds(0, 8), :] = vert
-            diff[term, pl.ds(8, 8), :] = hori
-            total[term] = value
+                slot = group * (2 * PAIRS) + o * PAIRS + p
+                beyond = meets * (rows[0][o][p : p + 1] if p < 8 else rows[1][o])
+                vert = diff_ref[slot, pl.ds(0, 8), :] - beyond
+                hori = diff_ref[slot, pl.ds(8, 8), :]
+                made.append((slot, vert, hori, start_ref[slot] - own_ref[pl.ds(slot, 1), :] * (coef_v * beyond)))
+        for slot, vert, hori, value in made:
+            diff[slot, pl.ds(0, 8), :] = vert
+            diff[slot, pl.ds(8, 8), :] = hori
+            total[slot] = value
         return carry
 
-    lax.fori_loop(0, groups, own, 0, unroll=4)
+    lax.fori_loop(0, groups, patch, 0, unroll=4)
+    copy.wait()
 
     def couple(step, carry):
         terms = [6 * step + i for i in range(6)]
         uppers, gains, mine = [], [], []
         for term in terms:
-            vert = diff[term, pl.ds(0, 8), :]
-            hori = diff[term, pl.ds(8, 8), :]
+            lower = places[term]
+            vert = diff[lower, pl.ds(0, 8), :]
+            hori = diff[lower, pl.ds(8, 8), :]
             parts = []
             for v in range(VARS):
                 coef_v = coef_ref[v + 1, pl.ds(0, 8), :]
                 coef_h = coef_ref[v + 1, pl.ds(8, 8), :]
-                upper = index_ref[slots + term * VARS + v]
+                upper = places[LOWER + term * VARS + v]
                 uppers.append(upper)
                 parts.append(
                     weight_ref[term, pl.ds(v, 1), :]
@@ -235,7 +253,8 @@
                 parts = [x + y for x, y in zip(parts[::2], parts[1::2])] + parts[len(parts) // 2 * 2 :]
             mine.append(parts[0])
         for i, term in enumerate(terms):
-            total[term] = total[term] + mine[i]
+            lower = places[term]
+            total[lower] = total[lower] + mine[i]
             sums = [total[uppers[i * VARS + v]] + gains[i * VARS + v] for v in range(VARS)]
             for v in range(VARS):
                 total[uppers[i * VARS + v]] = sums[v]
@@ -246,8 +265,8 @@
     def store(group, carry):
         made = []
         for p in range(PAIRS):
-            a = total[index_ref[group * (2 * PAIRS) + p]]
-            b = total[index_ref[group * (2 * PAIRS) + PAIRS + p]]
+            a = total[group * (2 * PAIRS) + p]
+            b = total[group * (2 * PAIRS) + PAIRS + p]
             made.append(jnp.where(low, a, b) + pltpu.roll(jnp.where(low, b, a), 64, 1))
         for p in range(PAIRS):
             out_ref[group, pl.ds(8 * p, 8), :] = made[p]
@@ -256,9 +275,14 @@
     lax.fori_loop(0, groups, store, 0, unroll=8)
 
 
-def unpack_kernel(got_ref, out_ref):
+def unpack_kernel(got_ref, result_ref, out_ref, sem):
     low = lanes_of() < 64
     mask, _ = here()
+
+    def send(r):
+        rows = pl.ds(8 * r, 8)
+        return pltpu.make_async_copy(out_ref.at[:, rows], result_ref.at[:, rows], sem.at[r])
+
     for r in range(4):
         for h in range(2):
             for p in range(PAIRS):
@@ -270,14 +294,17 @@
                 out_ref[p + PAIRS, pl.ds(8 * r, 8), pl.ds(128 * h, 128)] = jnp.where(
                     low, pltpu.roll(one, 64, 1), two
                 )
+        send(r).start()
+    for r in range(4):
+        send(r).wait()
 
 
 def vmem():
     return pl.BlockSpec(memory_space=pltpu.VMEM)
 
 
-def smem():
-    return pl.BlockSpec(memory_space=pltpu.SMEM)
+def hbm():
+    return pl.BlockSpec(memory_space=pltpu.HBM)
 
 
 def f32(*shape):
@@ -296,7 +323,11 @@
         pack_kernel,
         out_shape=f32(groups, ROWS, 128),
         in_specs=[vmem()],
-        out_specs=vmem(),
+        out_specs=hbm(),
+        scratch_shapes=[
+            pltpu.VMEM((groups, ROWS, 128), jnp.float32),
+            pltpu.SemaphoreType.DMA((groups,)),
+        ],
         compiler_params=PARAMS,
         cost_estimate=cost(2),
     )(fields)
@@ -317,40 +348,41 @@
     return pl.pallas_call(
         coef_kernel,
         out_shape=f32(modes.shape[0], 16, 128),
-        in_specs=[vmem(), vmem(), pl.BlockSpec(memory_space=pl.ANY)],
+        in_specs=[vmem(), vmem(), hbm()],
         out_specs=vmem(),
         compiler_params=PARAMS,
         cost_estimate=cost(1),
     )(modes, edge, weights)
 
 
-def load(index, got):
-    groups = got.shape[0]
+def load(own, got, coef):
+    slots = got.shape[0] * 2 * PAIRS
     return pl.pallas_call(
         load_kernel,
-        out_shape=f32(groups * 2 * PAIRS, 16, 128),
-        in_specs=[smem(), vmem()],
-        out_specs=vmem(),
+        out_shape=(f32(slots, 16, 128), f32(slots, 8, 128)),
+        in_specs=[vmem()] * 3,
+        out_specs=(vmem(), vmem()),
         compiler_params=PARAMS,
         cost_estimate=cost(4),
-    )(index, got)
-
-
-def mix(index, own, weights, diff, edge, coef):
+    )(own, got, coef)
+
+
+def mix(places, own, weights, diff, total, edge, coef):
     slots = diff.shape[0]
-    groups = slots // (2 * PAIRS)
     return pl.pallas_call(
         mix_kernel,
-        out_shape=f32(groups, BLOCK, 128),
-        in_specs=[smem(), smem()] + [vmem()] * 4,
+        out_shape=f32(slots // (2 * PAIRS), BLOCK, 128),
+        in_specs=[vmem()] * 7,
         out_specs=vmem(),
         scratch_shapes=[
             pltpu.VMEM((slots, 16, 128), jnp.float32),
             pltpu.VMEM((slots, 8, 128), jnp.float32),
+            pltpu.SMEM(places.shape, jnp.int32),
+            pltpu.SemaphoreType.DMA,
         ],
         compiler_params=PARAMS,
         cost_estimate=cost(5),
-    )(index, own, weights, diff, edge, coef)
+    )(places, own, weights, diff, total, edge, coef)
 
 
 def unpack(got, shape):
@@ -358,7 +390,8 @@
         unpack_kernel,
         out_shape=f32(*shape),
         in_specs=[vmem()],
-        out_specs=vmem(),
+        out_specs=hbm(),
+        scratch_shapes=[pltpu.VMEM(shape, jnp.float32), pltpu.SemaphoreType.DMA((4,))],
         compiler_params=PARAMS,
         cost_estimate=cost(1),
     )(got)
@@ -366,12 +399,14 @@
 
 def tables(pair_list, pair_value, assign):
     terms = assign.shape[0]
+    numbers = jnp.arange(terms, dtype=jnp.int32)
     row, col, mode = pair_list[:, 0:1], pair_list[:, 1:2], pair_list[:, 2:3]
-    at = jnp.minimum(row, col) == jnp.arange(terms, dtype=jnp.int32)[None, :]
+    slot = jnp.sum(jnp.where(col == assign[None, :], numbers[None, :], 0), axis=1, keepdims=True)
+    at = jnp.minimum(row, col) == numbers[None, :]
     kinds = jnp.arange(1 + 3 * VARS, dtype=jnp.int32)[None, :]
     wanted = jnp.where(kinds <= VARS, kinds, (kinds - 1) % VARS + 1)
     side = jnp.where(kinds <= VARS, row <= col, jnp.where(kinds <= 2 * VARS, row > col, row < col))
-    value = jnp.where(kinds <= 2 * VARS, pair_value[:, None], col.astype(jnp.float32))
+    value = jnp.where(kinds <= 2 * VARS, pair_value[:, None], slot.astype(jnp.float32))
     value = jnp.where((mode == wanted) & side, value, 0.0)
     found = lax.dot_general(
         at.astype(jnp.float32),
@@ -383,7 +418,10 @@
     coupled = jnp.pad(found[:LOWER, 1 : 1 + 2 * VARS], ((0, 0), (0, 4)))
     uppers = jnp.round(found[:LOWER, 1 + 2 * VARS :]).astype(jnp.int32).reshape(-1)
     weights = jnp.broadcast_to(coupled[:, :, None], coupled.shape + (128,))
-    return jnp.concatenate([assign, uppers]), found[:, 0], weights
+    held = assign[:, None] == numbers[None, :]
+    own = jnp.sum(jnp.where(held, found[:, 0][None, :], 0.0), axis=1, keepdims=True)
+    lowers = jnp.sum(jnp.where(held[:, :LOWER], numbers[:, None], 0), axis=0)
+    return jnp.concatenate([lowers, uppers]), jnp.broadcast_to(own, (terms, 128)), weights
 
 
 def shards(fields, modes, pair_list, pair_value, assign):
@@ -398,14 +436,14 @@
     sent = pack(fields, groups)
     sent, modes = lax.optimization_barrier((sent, modes))
     got = lax.all_to_all(sent, "term", 0, 0, tiled=True)
-    index, own, weights = tables(pair_list, pair_value, assign)
+    places, own, weights = tables(pair_list, pair_value, assign)
     _, place = here()
     edge = jnp.where(row_group(place) == 0, modes[:, 0], modes[:, modes.shape[1] - 1])
     coef = coefs(modes, lax.ppermute(edge, ("term", "space"), passes), weights)
-    got, coef, index = lax.optimization_barrier((got, coef, index))
+    got, coef, places, own = lax.optimization_barrier((got, coef, places, own))
     beyond = lax.ppermute(edges(got), ("term", "space"), passes)
-    diff = load(index, got)
-    mixed = mix(index, own, weights, diff, beyond, coef)
+    diff, total = load(own, got, coef)
+    mixed = mix(places, own, weights, diff, total, beyond, coef)
     back = lax.all_to_all(mixed, "term", 0, 0, tiled=True)
     return unpack(back, fields.shape)
 

time: 67.8 us -> 66.8 us (0.985)
  Pallas kernels: 8.98 us -> 7.54 us
  other arithmetic: 0.22 us -> 0.95 us
    pallas_call x2, Pallas kernels: 6.13 us -> 4.79 us  [the longest x1 2.65 us: mix(): pl.pallas_call(mix_kernel, out_shape=f32(slots // (2 * PAIRS), BLOCK, 128...]
    all_to_all x1, waiting for transfers between devices: 9.94 us -> 9.16 us  [shards(): got = lax.all_to_all(sent, 'term', 0, 0, tiled=True)]
  transfers between devices with their start and end apart: 3 -> 3, of which waited for: 2 -> 2; matrix products, arithmetic and copies ran while one was open for 6% -> 7% of each run, Pallas kernels for 4% -> 4%
where the time goes in v3:
time: 66.8 us; the launch traced here: 66.5 us
  blocking collectives  22.3 us (33%)
  starting transfers between devices  19.6 us (29%)
  waiting for transfers between devices  10.6 us (16%)
  Pallas kernels  7.54 us (11%)
  matrix products  3.15 us (5%)
  local copies, waits for them, and re-layouts  2.09 us (3%)
  other arithmetic  0.95 us (1%)
    all_to_all x1, blocking collectives, shards(): back = lax.all_to_all(mixed, 'term', 0, 0, tiled=True)  22.3 us
    all_to_all x1, waiting for transfers between devices, shards(): got = lax.all_to_all(sent, 'term', 0, 0, tiled=True)  9.16 us
    all_to_all x1, starting transfers between devices, shards(): got = lax.all_to_all(sent, 'term', 0, 0, tiled=True)  8.48 us
    ppermute x1, starting transfers between devices, shards(): coef = coefs(modes, lax.ppermute(edge, ('term', 'space'), passes), weights)  5.64 us
    ppermute x1, starting transfers between devices, shards(): beyond = lax.ppermute(edges(got), ('term', 'space'), passes)  5.53 us
    dot_general x1, matrix products, tables(): lax.dot_general(at.astype(jnp.float32), value, (((0,), (0,)), ((), ())),...  3.15 us
    pallas_call x1, Pallas kernels, mix(): pl.pallas_call(mix_kernel, out_shape=f32(slots // (2 * PAIRS), BLOCK, 128...  2.65 us
    pallas_call x1, Pallas kernels, load(): pl.pallas_call(load_kernel, out_shape=(f32(slots, 16, 128), f32(slots, 8,...  2.15 us
  transfers between devices with their start and end apart: 3, of which 2 were waited for; matrix products, arithmetic and copies ran while one was open for 7% of the time, Pallas kernels for 4%

profile of v3, /device:TPU:16, one launch (start us, length us, event | category | flops | bytes accessed | tf_op | source)
XLA Modules:
  0.0 66.5 jit_solution(14978959475190097116)
XLA Ops:
  0.0 1.1 %copy-done.1 = f32[18,32,256]{2,1,0:T(8,128)S(1)} copy-done((f32[18,32,256]{2,1,0:T(8,128)S(1)}, f32[18,32,256]{2,1,0:T(8,128)}, u32[]{:S(2)}) %copy-start.1) | copy-done | bytes 589848
  1.1 1.6 %shard_map.55 = f32[16,96,128]{2,1,0:T(8,128)} custom-call(f32[18,32,256]{2,1,0:T(8,128)S(1)} %copy-done.1), custom_call_target="tpu_custom_call" | custom-call | bytes 6000000 | tf_op jit(solution)/shard_map/pallas_call | solution.py:322
  2.7 8.5 %all-to-all-start = ((f32[16,96,128]{2,1,0:T(8,128)}), f32[16,96,128]{2,1,0:T(8,128)S(1)}, u32[]{:S(2)}, u32[]{:S(2)}) async-start(f32[16,96,128]{2,1,0:T(8,128)} %shard_map.55), calls=%async_computation | async-start | bytes 1572864 | tf_op jit(solution)/shard_map/all_to_all | solution.py:438
  11.2 0.2 copy.13
  11.5 5.6 %collective-permute-start = (f32[11,256]{1,0:T(8,128)S(1)}, f32[11,256]{1,0:T(8,128)S(1)}, u32[]{:S(2)}, u32[]{:S(2)}) collective-permute-start(f32[11,256]{1,0:T(8,128)S(1)} %fusion.18), channel_id=1, source_target_pairs={{49,48},{48,49},{130,1},{1,130},{179,178},{178,179},{4,131},{131,4... | collective-permute-start | bytes 33800 | tf_op jit(solution)/shard_map/ppermute | solution.py:442
  17.2 0.3 select_reduce_fusion
  17.5 0.1 compare_reduce_fusion.1
  17.6 3.1 %fusion = f32[288,31]{0,1:T(8,128)S(1)} fusion(s32[2048]{0:T(1024)S(1)} %bitcast.7, f32[2048]{0:T(1024)S(1)} %convert_element_type.14, f32[2048]{0:T(1024)S(1)} %copy-done.4, s32[31]{0:T(128)S(1)} %iota_select_fusion, s32[2048]{0:T(1024)S(1)} %bitcast.6, pred[2048]{0:T(1024)(128)(4,1)S(1)} %get-tuple-element.22, pred[31]{0:T(512)(128)(4,1)S(1)} %get-tuple-element.28, ...), kind=kOutput, calls=%fused_computation.1 | convolution fusion | flops 220385280 | bytes 74810 | tf_op jit(solution)/shard_map/dot_general | solution.py:411
  20.8 0.1 copy.17
  20.9 0.1 reshape.48
  21.1 0.1 iota_compare_fusion.2
  21.3 0.2 select_reduce_fusion.1
  21.5 0.1 pad_add_fusion.place_ref
  21.6 0.1 copy.19
  21.7 0.3 broadcast_in_dim.143.weight_ref
  22.0 0.2 shard_map.56.coef_ref
  22.2 9.2 %all-to-all-done.got_ref = f32[16,96,128]{2,1,0:T(8,128)S(1)} async-done(((f32[16,96,128]{2,1,0:T(8,128)}), f32[16,96,128]{2,1,0:T(8,128)S(1)}, u32[]{:S(2)}, u32[]{:S(2)}) %all-to-all-start) | async-done | bytes 786464 | tf_op jit(solution)/shard_map/all_to_all | solution.py:438
  31.3 0.1 broadcast_in_dim.149.own_ref
  31.4 5.5 %collective-permute-start.1 = (f32[144,128]{1,0:T(8,128)S(1)}, f32[144,128]{1,0:T(8,128)S(1)}, u32[]{:S(2)}, u32[]{:S(2)}) collective-permute-start(f32[144,128]{1,0:T(8,128)S(1)} %shard_map.58), channel_id=1, source_target_pairs={{49,48},{48,49},{130,1},{1,130},{179,178},{178,179},{4,131},{131,4... | collective-permute-start | bytes 221192 | tf_op jit(solution)/shard_map/ppermute | solution.py:444
  37.0 2.1 %shard_map.57 = (f32[288,16,128]{2,1,0:T(8,128)S(1)}, f32[288,8,128]{2,1,0:T(8,128)S(1)}) custom-call(f32[288,128]{1,0:T(8,128)S(1)} %broadcast_in_dim.149.own_ref, f32[16,96,128]{2,1,0:T(8,128)S(1)} %all-to-all-done.got_ref, f32[11,16,128]{2,1,0:T(8,128)S(1)} %shard_map.56.coef_ref), custom_call_target="tpu_custom_call" | custom-call | bytes 12000000 | tf_op jit(solution)/shard_map/pallas_call | solution.py:360
  39.1 1.4 %collective-permute-done.1.edge_ref = f32[144,128]{1,0:T(8,128)S(1)} collective-permute-done((f32[144,128]{1,0:T(8,128)S(1)}, f32[144,128]{1,0:T(8,128)S(1)}, u32[]{:S(2)}, u32[]{:S(2)}) %collective-permute-start.1) | collective-permute-done | bytes 73760 | tf_op jit(solution)/shard_map/ppermute | solution.py:444
  40.6 2.6 %shard_map.59 = f32[16,72,128]{2,1,0:T(8,128)S(1)} custom-call(s32[726]{0:T(1024)S(1)} %pad_add_fusion.place_ref, f32[288,128]{1,0:T(8,128)S(1)} %broadcast_in_dim.149.own_ref, f32[66,24,128]{2,1,0:T(8,128)S(1)} %broadcast_in_dim.143.weight_ref, f32[288,16,128]{2,1,0:T(8,128)S(1)} %get-tuple-element.19.diff_ref, ...), custom_call_target="tpu_custom_call" | custom-call | bytes 15000000 | tf_op jit(solution)/shard_map/pallas_call | solution.py:372
  43.2 22.3 %all_to_all.10.got_ref = f32[16,72,128]{2,1,0:T(8,128)S(1)} all-to-all(f32[16,72,128]{2,1,0:T(8,128)S(1)} %shard_map.59), channel_id=1, replica_groups=mesh['term'=16,'space'=16] {'term'}, dimensions={0} | all-to-all | bytes 1179648 | tf_op jit(solution)/shard_map/all_to_all | solution.py:447
  65.6 1.0 %shard_map.60 = f32[18,32,256]{2,1,0:T(8,128)} custom-call(f32[16,72,128]{2,1,0:T(8,128)S(1)} %all_to_all.10.got_ref), custom_call_target="tpu_custom_call" | custom-call | bytes 3000000 | tf_op jit(solution)/shard_map/pallas_call | solution.py:389
  (21 shorter events, 0.2 us)
Async XLA Ops:
  0.0 11.2 %copy-start = (f32[11,32,256]{2,1,0:T(8,128)S(1)}, f32[11,32,256]{2,1,0:T(8,128)}, u32[]{:S(2)}) copy-start(f32[11,32,256]{2,1,0:T(8,128)} %modes_ref) | copy-start | bytes 1081348
  0.0 1.1 %copy-start.1 = (f32[18,32,256]{2,1,0:T(8,128)S(1)}, f32[18,32,256]{2,1,0:T(8,128)}, u32[]{:S(2)}) copy-start(f32[18,32,256]{2,1,0:T(8,128)} %f_ref.1) | copy-start | bytes 1769476
  1.1 16.0 %copy-start.2 = (s32[2048,3]{0,1:T(4,128)S(1)}, s32[2048,3]{0,1:T(4,128)}, u32[]{:S(2)}) copy-start(s32[2048,3]{0,1:T(4,128)} %param.7) | copy-start | bytes 73732
  1.1 16.0 %copy-start.3 = (s32[288]{0:T(512)S(1)}, s32[288]{0:T(512)}, u32[]{:S(2)}) copy-start(s32[288]{0:T(512)} %param.9) | copy-start | bytes 3460
  1.1 16.5 %copy-start.4 = (f32[2048]{0:T(1024)S(1)}, f32[2048]{0:T(1024)}, u32[]{:S(2)}) copy-start(f32[2048]{0:T(1024)} %param.8) | copy-start | bytes 24580
  2.7 28.6 %all-to-all-start = ((f32[16,96,128]{2,1,0:T(8,128)}), f32[16,96,128]{2,1,0:T(8,128)S(1)}, u32[]{:S(2)}, u32[]{:S(2)}) async-start(f32[16,96,128]{2,1,0:T(8,128)} %shard_map.55), calls=%async_computation | async-start | bytes 1572864 | tf_op jit(solution)/shard_map/all_to_all | solution.py:438
  11.5 10.2 %collective-permute-start = (f32[11,256]{1,0:T(8,128)S(1)}, f32[11,256]{1,0:T(8,128)S(1)}, u32[]{:S(2)}, u32[]{:S(2)}) collective-permute-start(f32[11,256]{1,0:T(8,128)S(1)} %fusion.18), channel_id=1, source_target_pairs={{49,48},{48,49},{130,1},{1,130},{179,178},{178,179},{4,131},{131,4... | collective-permute-start | bytes 33800 | tf_op jit(solution)/shard_map/ppermute | solution.py:442
  31.4 9.1 %collective-permute-start.1 = (f32[144,128]{1,0:T(8,128)S(1)}, f32[144,128]{1,0:T(8,128)S(1)}, u32[]{:S(2)}, u32[]{:S(2)}) collective-permute-start(f32[144,128]{1,0:T(8,128)S(1)} %shard_map.58), channel_id=1, source_target_pairs={{49,48},{48,49},{130,1},{1,130},{179,178},{178,179},{4,131},{131,4... | collective-permute-start | bytes 221192 | tf_op jit(solution)/shard_map/ppermute | solution.py:444

commit v4 on v3

--- a/solution.py
+++ b/solution.py
@@ -19,6 +19,10 @@
     return 4 * c + (r ^ c)
 
 
+def rank(device):
+    return (device & 1) << 3 | (device & 2) << 1 | (device & 4) >> 1 | (device >> 3 ^ 1)
+
+
 def mask_at(space):
     return (space >> 1 & 1) * 8 + (space & 1) * 3
 
@@ -48,7 +52,7 @@
     mask, _ = here()
 
     def send(r, c):
-        to = holder(r, c) ^ mask
+        to = rank(holder(r, c) ^ mask)
         return pltpu.make_async_copy(out_ref.at[to], sent_ref.at[to], out_sem.at[4 * r + c])
 
     for r in range(4):
@@ -66,15 +70,15 @@
                 for o in range(2):
                     c = 2 * h + o
                     first, last = both[o][0:1], both[o][7:8]
-                    out_ref[holder(r, c) ^ mask, pl.ds(8 * p, 8), :] = both[o]
+                    out_ref[rank(holder(r, c) ^ mask), pl.ds(8 * p, 8), :] = both[o]
                     if r == 0:
-                        out_ref[holder(0, c) ^ mask, pl.ds(FIRST + p, 1), :] = first
+                        out_ref[rank(holder(0, c) ^ mask), pl.ds(FIRST + p, 1), :] = first
                     if r == 3:
-                        out_ref[holder(3, c) ^ mask, pl.ds(FIRST + p, 1), :] = last
+                        out_ref[rank(holder(3, c) ^ mask), pl.ds(FIRST + p, 1), :] = last
                     if r < 3:
-                        out_ref[holder(r + 1, c) ^ mask, pl.ds((FIRST if r < 2 else SECOND) + p, 1), :] = last
+                        out_ref[rank(holder(r + 1, c) ^ mask), pl.ds((FIRST if r < 2 else SECOND) + p, 1), :] = last
                     if r > 0:
-                        out_ref[holder(r - 1, c) ^ mask, pl.ds(SECOND + p, 1), :] = first
+                        out_ref[rank(holder(r - 1, c) ^ mask), pl.ds(SECOND + p, 1), :] = first
                 pair = (lane % 64) // 2 == p
                 ga = jnp.where(pair, pltpu.roll(a, (2 * p - 63) % 128, 1), ga)
                 gb = jnp.where(pair, pltpu.roll(b, 2 * p + 1, 1), gb)
@@ -90,7 +94,7 @@
         for c in range(4):
             moved = pltpu.roll(pltpu.roll(sides[c], 32, 1), 2, 0)
             kept = jnp.where(spare, moved, sides[c])
-            out_ref[holder(r, c) ^ mask, pl.ds(SIDE, 6), :] = kept[0:6]
+            out_ref[rank(holder(r, c) ^ mask), pl.ds(SIDE, 6), :] = kept[0:6]
         for done in ((r - 1, r) if r == 3 else (r - 1,)):
             if done >= 0:
                 for c in range(4):
@@ -286,8 +290,8 @@
     for r in range(4):
         for h in range(2):
             for p in range(PAIRS):
-                one = got_ref[holder(r, 2 * h) ^ mask, pl.ds(8 * p, 8), :]
-                two = got_ref[holder(r, 2 * h + 1) ^ mask, pl.ds(8 * p, 8), :]
+                one = got_ref[rank(holder(r, 2 * h) ^ mask), pl.ds(8 * p, 8), :]
+                two = got_ref[rank(holder(r, 2 * h + 1) ^ mask), pl.ds(8 * p, 8), :]
                 out_ref[p, pl.ds(8 * r, 8), pl.ds(128 * h, 128)] = jnp.where(
                     low, one, pltpu.roll(two, 64, 1)
                 )
@@ -421,7 +425,8 @@
     held = assign[:, None] == numbers[None, :]
     own = jnp.sum(jnp.where(held, found[:, 0][None, :], 0.0), axis=1, keepdims=True)
     lowers = jnp.sum(jnp.where(held[:, :LOWER], numbers[:, None], 0), axis=0)
-    return jnp.concatenate([lowers, uppers]), jnp.broadcast_to(own, (terms, 128)), weights
+    places = jnp.pad(jnp.concatenate([lowers, uppers]), (0, 1024 - LOWER * (1 + VARS)))
+    return places, jnp.broadcast_to(own, (terms, 128)), weights
 
 
 def shards(fields, modes, pair_list, pair_value, assign):
@@ -433,9 +438,11 @@
             lower = (holder(0, c) ^ mask_at(s + 1)) * count + s + 1
             upper = (holder(3, c) ^ mask_at(s)) * count + s
             passes += [(lower, upper), (upper, lower)]
+    order = sorted(range(groups), key=rank)
+    assign = assign.reshape(groups, -1)[jnp.array(order)].reshape(-1)
     sent = pack(fields, groups)
     sent, modes = lax.optimization_barrier((sent, modes))
-    got = lax.all_to_all(sent, "term", 0, 0, tiled=True)
+    got = lax.all_to_all(sent, "term", 0, 0, axis_index_groups=[order], tiled=True)
     places, own, weights = tables(pair_list, pair_value, assign)
     _, place = here()
     edge = jnp.where(row_group(place) == 0, modes[:, 0], modes[:, modes.shape[1] - 1])
@@ -444,7 +451,7 @@
     beyond = lax.ppermute(edges(got), ("term", "space"), passes)
     diff, total = load(own, got, coef)
     mixed = mix(places, own, weights, diff, total, beyond, coef)
-    back = lax.all_to_all(mixed, "term", 0, 0, tiled=True)
+    back = lax.all_to_all(mixed, "term", 0, 0, axis_index_groups=[order], tiled=True)
     return unpack(back, fields.shape)
 
 

time: 66.8 us -> 63.7 us (0.954)
  starting transfers between devices: 19.6 us -> 14.5 us
  waiting for transfers between devices: 10.6 us -> 14.5 us
  blocking collectives: 22.3 us -> 19.7 us
  local copies, waits for them, and re-layouts: 2.09 us -> 2.82 us
    ppermute x1, starting transfers between devices: 5.53 us -> 1.92 us  [shards(): beyond = lax.ppermute(edges(got), ('term', 'space'), passes)]
    ppermute x1, waiting for transfers between devices: 1.43 us -> 4.6 us  [shards(): beyond = lax.ppermute(edges(got), ('term', 'space'), passes)]
    all_to_all x1, blocking collectives: 22.3 us -> 19.7 us  [shards(): lax.all_to_all(mixed, 'term', 0, 0, axis_index_groups=[order], tiled=True)]
    ppermute x1, starting transfers between devices: 5.64 us -> 3.63 us  [shards(): coef = coefs(modes, lax.ppermute(edge, ('term', 'space'), passes), weights)]
    all_to_all x1, waiting for transfers between devices: 9.16 us -> 9.9 us  [shards(): lax.all_to_all(sent, 'term', 0, 0, axis_index_groups=[order], tiled=True)]
  transfers between devices with their start and end apart: 3 -> 3, of which waited for: 2 -> 2; matrix products, arithmetic and copies ran while one was open for 7% -> 9% of each run, Pallas kernels for 4% -> 4%
where the time goes in v4:
time: 63.7 us; the launch traced here: 63.4 us
  blocking collectives  19.7 us (31%)
  starting transfers between devices  14.5 us (23%)
  waiting for transfers between devices  14.5 us (23%)
  Pallas kernels  7.55 us (12%)
  matrix products  3.15 us (5%)
  local copies, waits for them, and re-layouts  2.82 us (4%)
  other arithmetic  0.96 us (2%)
    all_to_all x1, blocking collectives, shards(): lax.all_to_all(mixed, 'term', 0, 0, axis_index_groups=[order], tiled=True)  19.7 us
    all_to_all x1, waiting for transfers between devices, shards(): lax.all_to_all(sent, 'term', 0, 0, axis_index_groups=[order], tiled=True)  9.9 us
    all_to_all x1, starting transfers between devices, shards(): lax.all_to_all(sent, 'term', 0, 0, axis_index_groups=[order], tiled=True)  8.95 us
    ppermute x1, waiting for transfers between devices, shards(): beyond = lax.ppermute(edges(got), ('term', 'space'), passes)  4.6 us
    ppermute x1, starting transfers between devices, shards(): coef = coefs(modes, lax.ppermute(edge, ('term', 'space'), passes), weights)  3.63 us
    dot_general x1, matrix products, tables(): lax.dot_general(at.astype(jnp.float32), value, (((0,), (0,)), ((), ())),...  3.15 us
    pallas_call x1, Pallas kernels, mix(): pl.pallas_call(mix_kernel, out_shape=f32(slots // (2 * PAIRS), BLOCK, 128...  2.65 us
    pallas_call x1, Pallas kernels, load(): pl.pallas_call(load_kernel, out_shape=(f32(slots, 16, 128), f32(slots, 8,...  2.15 us
  transfers between devices with their start and end apart: 3, of which 2 were waited for; matrix products, arithmetic and copies ran while one was open for 9% of the time, Pallas kernels for 4%

profile of v4, /device:TPU:16, one launch (start us, length us, event | category | flops | bytes accessed | tf_op | source)
XLA Modules:
  0.0 63.4 jit_solution(597091753010917155)
XLA Ops:
  0.0 1.1 %copy-done.1 = f32[18,32,256]{2,1,0:T(8,128)S(1)} copy-done((f32[18,32,256]{2,1,0:T(8,128)S(1)}, f32[18,32,256]{2,1,0:T(8,128)}, u32[]{:S(2)}) %copy-start.1) | copy-done | bytes 589848
  1.1 1.6 %shard_map.64 = f32[16,96,128]{2,1,0:T(8,128)} custom-call(f32[18,32,256]{2,1,0:T(8,128)S(1)} %copy-done.1), custom_call_target="tpu_custom_call" | custom-call | bytes 6000000 | tf_op jit(solution)/shard_map/pallas_call | solution.py:326
  2.7 8.9 %all-to-all-start = ((f32[16,96,128]{2,1,0:T(8,128)}), f32[16,96,128]{2,1,0:T(8,128)S(1)}, u32[]{:S(2)}, u32[]{:S(2)}) async-start(f32[16,96,128]{2,1,0:T(8,128)} %shard_map.64), calls=%async_computation | async-start | bytes 1572864 | tf_op jit(solution)/shard_map/all_to_all | solution.py:445
  11.7 0.2 copy.14
  11.9 3.6 %collective-permute-start = (f32[11,256]{1,0:T(8,128)S(1)}, f32[11,256]{1,0:T(8,128)S(1)}, u32[]{:S(2)}, u32[]{:S(2)}) collective-permute-start(f32[11,256]{1,0:T(8,128)S(1)} %fusion.18), channel_id=1, source_target_pairs={{49,48},{48,49},{130,1},{1,130},{179,178},{178,179},{4,131},{131,4... | collective-permute-start | bytes 33800 | tf_op jit(solution)/shard_map/ppermute | solution.py:449
  15.7 0.6 gather_fusion
  16.3 0.1 eq.78
  16.4 0.3 select_reduce_fusion
  16.9 3.2 %fusion = f32[288,31]{0,1:T(8,128)S(1)} fusion(s32[2048]{0:T(1024)S(1)} %bitcast.7, f32[2048]{0:T(1024)S(1)} %convert_element_type.14, f32[2048]{0:T(1024)S(1)} %copy-done.5, s32[31]{0:T(128)S(1)} %iota_select_fusion, s32[2048]{0:T(1024)S(1)} %bitcast.6, pred[2048]{0:T(1024)(128)(4,1)S(1)} %get-tuple-element.22, pred[31]{0:T(512)(128)(4,1)S(1)} %get-tuple-element.28, ...), kind=kOutput, calls=%fused_computation.2 | convolution fusion | flops 220385280 | bytes 74810 | tf_op jit(solution)/shard_map/dot_general | solution.py:415
  20.0 0.1 copy.18
  20.1 0.1 reshape.52
  20.3 0.1 iota_compare_fusion.2
  20.5 0.2 select_reduce_fusion.1
  20.8 0.1 copy.20
  20.9 0.3 broadcast_in_dim.145.weight_ref
  21.2 0.2 shard_map.65.coef_ref
  21.4 9.9 %all-to-all-done.got_ref = f32[16,96,128]{2,1,0:T(8,128)S(1)} async-done(((f32[16,96,128]{2,1,0:T(8,128)}), f32[16,96,128]{2,1,0:T(8,128)S(1)}, u32[]{:S(2)}, u32[]{:S(2)}) %all-to-all-start) | async-done | bytes 786464 | tf_op jit(solution)/shard_map/all_to_all | solution.py:445
  31.3 0.1 broadcast_in_dim.151.own_ref
  31.4 1.9 %collective-permute-start.1 = (f32[144,128]{1,0:T(8,128)S(1)}, f32[144,128]{1,0:T(8,128)S(1)}, u32[]{:S(2)}, u32[]{:S(2)}) collective-permute-start(f32[144,128]{1,0:T(8,128)S(1)} %shard_map.67), channel_id=1, source_target_pairs={{49,48},{48,49},{130,1},{1,130},{179,178},{178,179},{4,131},{131,4... | collective-permute-start | bytes 221192 | tf_op jit(solution)/shard_map/ppermute | solution.py:451
  33.4 2.1 %shard_map.66 = (f32[288,16,128]{2,1,0:T(8,128)S(1)}, f32[288,8,128]{2,1,0:T(8,128)S(1)}) custom-call(f32[288,128]{1,0:T(8,128)S(1)} %broadcast_in_dim.151.own_ref, f32[16,96,128]{2,1,0:T(8,128)S(1)} %all-to-all-done.got_ref, f32[11,16,128]{2,1,0:T(8,128)S(1)} %shard_map.65.coef_ref), custom_call_target="tpu_custom_call" | custom-call | bytes 12000000 | tf_op jit(solution)/shard_map/pallas_call | solution.py:364
  35.5 4.6 %collective-permute-done.1.edge_ref = f32[144,128]{1,0:T(8,128)S(1)} collective-permute-done((f32[144,128]{1,0:T(8,128)S(1)}, f32[144,128]{1,0:T(8,128)S(1)}, u32[]{:S(2)}, u32[]{:S(2)}) %collective-permute-start.1) | collective-permute-done | bytes 73760 | tf_op jit(solution)/shard_map/ppermute | solution.py:451
  40.1 2.6 %shard_map.68 = f32[16,72,128]{2,1,0:T(8,128)S(1)} custom-call(s32[1024]{0:T(1024)S(1)} %pad.9.place_ref, f32[288,128]{1,0:T(8,128)S(1)} %broadcast_in_dim.151.own_ref, f32[66,24,128]{2,1,0:T(8,128)S(1)} %broadcast_in_dim.145.weight_ref, f32[288,16,128]{2,1,0:T(8,128)S(1)} %get-tuple-element.19.diff_ref, f32[288,8,128]{2,1,0:T(8,128)S(1)} %get-tuple-element.20.start_ref, ...), custom_call_target="tpu_custom_call" | custom-call | bytes 15000000 | tf_op jit(solution)/shard_map/pallas_call | solution.py:376
  42.8 19.7 %all_to_all.10.got_ref = f32[16,72,128]{2,1,0:T(8,128)S(1)} all-to-all(f32[16,72,128]{2,1,0:T(8,128)S(1)} %shard_map.68), channel_id=1, replica_groups={{128,0,192,64,160,32,224,96,144,16,208,80,176,48,240,112},{129,1,193,65..., dimensions={0} | all-to-all | bytes 1179648 | tf_op jit(solution)/shard_map/all_to_all | solution.py:454
  62.5 0.9 %shard_map.69 = f32[18,32,256]{2,1,0:T(8,128)} custom-call(f32[16,72,128]{2,1,0:T(8,128)S(1)} %all_to_all.10.got_ref), custom_call_target="tpu_custom_call" | custom-call | bytes 3000000 | tf_op jit(solution)/shard_map/pallas_call | solution.py:393
  (28 shorter events, 0.4 us)
Async XLA Ops:
  0.0 15.7 %copy-start.4 = (s32[16]{0:T(128)S(1)}, s32[16]{0:T(128)}, u32[]{:S(2)}) copy-start(s32[16]{0:T(128)} %constant.52) | copy-start | bytes 196
  0.0 11.7 %copy-start = (f32[11,32,256]{2,1,0:T(8,128)S(1)}, f32[11,32,256]{2,1,0:T(8,128)}, u32[]{:S(2)}) copy-start(f32[11,32,256]{2,1,0:T(8,128)} %modes_ref) | copy-start | bytes 1081348
  0.0 1.1 %copy-start.1 = (f32[18,32,256]{2,1,0:T(8,128)S(1)}, f32[18,32,256]{2,1,0:T(8,128)}, u32[]{:S(2)}) copy-start(f32[18,32,256]{2,1,0:T(8,128)} %f_ref.1) | copy-start | bytes 1769476
  1.1 14.5 %copy-start.2 = (s32[2048,3]{0,1:T(4,128)S(1)}, s32[2048,3]{0,1:T(4,128)}, u32[]{:S(2)}) copy-start(s32[2048,3]{0,1:T(4,128)} %param.8) | copy-start | bytes 73732
  1.1 14.5 %copy-start.3 = (s32[288]{0:T(512)S(1)}, s32[288]{0:T(512)}, u32[]{:S(2)}) copy-start(s32[288]{0:T(512)} %param.10) | copy-start | bytes 3460
  1.1 15.7 %copy-start.5 = (f32[2048]{0:T(1024)S(1)}, f32[2048]{0:T(1024)}, u32[]{:S(2)}) copy-start(f32[2048]{0:T(1024)} %param.9) | copy-start | bytes 24580
  2.7 28.6 %all-to-all-start = ((f32[16,96,128]{2,1,0:T(8,128)}), f32[16,96,128]{2,1,0:T(8,128)S(1)}, u32[]{:S(2)}, u32[]{:S(2)}) async-start(f32[16,96,128]{2,1,0:T(8,128)} %shard_map.64), calls=%async_computation | async-start | bytes 1572864 | tf_op jit(solution)/shard_map/all_to_all | solution.py:445
  11.9 9.0 %collective-permute-start = (f32[11,256]{1,0:T(8,128)S(1)}, f32[11,256]{1,0:T(8,128)S(1)}, u32[]{:S(2)}, u32[]{:S(2)}) collective-permute-start(f32[11,256]{1,0:T(8,128)S(1)} %fusion.18), channel_id=1, source_target_pairs={{49,48},{48,49},{130,1},{1,130},{179,178},{178,179},{4,131},{131,4... | collective-permute-start | bytes 33800 | tf_op jit(solution)/shard_map/ppermute | solution.py:449
  31.4 8.7 %collective-permute-start.1 = (f32[144,128]{1,0:T(8,128)S(1)}, f32[144,128]{1,0:T(8,128)S(1)}, u32[]{:S(2)}, u32[]{:S(2)}) collective-permute-start(f32[144,128]{1,0:T(8,128)S(1)} %shard_map.67), channel_id=1, source_target_pairs={{49,48},{48,49},{130,1},{1,130},{179,178},{178,179},{4,131},{131,4... | collective-permute-start | bytes 221192 | tf_op jit(solution)/shard_map/ppermute | solution.py:451

commit v5 on v4

--- a/solution.py
+++ b/solution.py
@@ -7,10 +7,9 @@
 
 PAIRS = 9
 BLOCK = 8 * PAIRS
-ROWS = 96
-FIRST = 72
-SECOND = 81
-SIDE = 90
+ROWS = 88
+HALO = 72
+SIDE = 81
 LOWER = 66
 VARS = 10
 
@@ -71,14 +70,10 @@
                     c = 2 * h + o
                     first, last = both[o][0:1], both[o][7:8]
                     out_ref[rank(holder(r, c) ^ mask), pl.ds(8 * p, 8), :] = both[o]
-                    if r == 0:
-                        out_ref[rank(holder(0, c) ^ mask), pl.ds(FIRST + p, 1), :] = first
-                    if r == 3:
-                        out_ref[rank(holder(3, c) ^ mask), pl.ds(FIRST + p, 1), :] = last
-                    if r < 3:
-                        out_ref[rank(holder(r + 1, c) ^ mask), pl.ds((FIRST if r < 2 else SECOND) + p, 1), :] = last
-                    if r > 0:
-                        out_ref[rank(holder(r - 1, c) ^ mask), pl.ds(SECOND + p, 1), :] = first
+                    if r % 2 == 0:
+                        out_ref[rank(holder(r + 1, c) ^ mask), pl.ds(HALO + p, 1), :] = last
+                    else:
+                        out_ref[rank(holder(r - 1, c) ^ mask), pl.ds(HALO + p, 1), :] = first
                 pair = (lane % 64) // 2 == p
                 ga = jnp.where(pair, pltpu.roll(a, (2 * p - 63) % 128, 1), ga)
                 gb = jnp.where(pair, pltpu.roll(b, 2 * p + 1, 1), gb)
@@ -94,9 +89,9 @@
         for c in range(4):
             moved = pltpu.roll(pltpu.roll(sides[c], 32, 1), 2, 0)
             kept = jnp.where(spare, moved, sides[c])
-            out_ref[rank(holder(r, c) ^ mask), pl.ds(SIDE, 6), :] = kept[0:6]
-        for done in ((r - 1, r) if r == 3 else (r - 1,)):
-            if done >= 0:
+            out_ref[rank(holder(r, c) ^ mask), pl.ds(SIDE, 7), :] = kept[0:7]
+        for done in (r - 1, r):
+            if r % 2 == 1:
                 for c in range(4):
                     send(done, c).start()
     for r in range(4):
@@ -105,10 +100,16 @@
 
 
 def edge_kernel(got_ref, edge_ref):
+    _, place = here()
     groups = got_ref.shape[0]
-    for group in range(groups):
-        edge_ref[pl.ds(8 * group, 8), :] = got_ref[group, pl.ds(FIRST, 8), :]
-        edge_ref[pl.ds(8 * groups + group, 1), :] = got_ref[group, pl.ds(FIRST + 8, 1), :]
+    even = row_group(place) % 2 == 0
+    for row, wanted in ((0, even), (7, jnp.logical_not(even))):
+
+        @pl.when(wanted)
+        def _():
+            for group in range(groups):
+                edge_ref[pl.ds(8 * group, 8), :] = got_ref[group, pl.ds(row, 8, stride=8), :]
+                edge_ref[pl.ds(8 * groups + group, 1), :] = got_ref[group, pl.ds(64 + row, 1), :]
 
 
 def coef_kernel(modes_ref, edge_ref, weight_ref, coef_ref):
@@ -152,27 +153,23 @@
     _, place = here()
     lane, sub = lanes_of(), subs_of()
     low = lane < 64
-    block_row = row_group(place)
-    first = block_row == 0
-    last = block_row == 3
-    over_one = (sub == 0) & jnp.logical_not(first | last)
-    over_two = (sub == 0) & last
-    under = (sub == 7) & jnp.logical_not(last)
+    even = row_group(place) % 2 == 0
+    over = (sub == 0) & jnp.logical_not(even)
+    under = (sub == 7) & even
     inner_up = sub > 0
     inner_down = sub < 7
 
     def load(group, carry):
         tail = got_ref[group, pl.ds(ROWS - 8, 8), :]
         beside = jnp.where(
-            sub < 6, pltpu.roll(tail, 6, 0), pltpu.roll(pltpu.roll(tail, 96, 1), 4, 0)
+            sub < 6, pltpu.roll(tail, 7, 0), pltpu.roll(pltpu.roll(tail, 96, 1), 5, 0)
         )
         made = []
         for p in range(PAIRS):
             cells = got_ref[group, pl.ds(8 * p, 8), :]
-            one = got_ref[group, pl.ds(FIRST + p, 1), :]
-            two = got_ref[group, pl.ds(SECOND + p, 1), :]
-            above = jnp.where(over_one, one, jnp.where(over_two, two, 0.0))
-            below = jnp.where(under, two, 0.0)
+            halo = got_ref[group, pl.ds(HALO + p, 1), :]
+            above = jnp.where(over, halo, 0.0)
+            below = jnp.where(under, halo, 0.0)
             up = cells - jnp.where(inner_up, pltpu.roll(cells, 1, 0), above)
             down = cells - jnp.where(inner_down, pltpu.roll(cells, 7, 0), below)
             left = cells - jnp.where(
@@ -206,9 +203,10 @@
     lane, sub = lanes_of(), subs_of()
     low = lane < 64
     groups = out_ref.shape[0]
-    first = row_group(place) == 0
-    last = row_group(place) == 3
-    meets = jnp.where((low & (sub == 0) & first) | ((lane >= 64) & (sub == 7) & last), 1.0, 0.0)
+    even = row_group(place) % 2 == 0
+    meets = jnp.where(
+        (low & (sub == 0) & even) | ((lane >= 64) & (sub == 7) & jnp.logical_not(even)), 1.0, 0.0
+    )
 
     def patch(group, carry):
         edge = edge_ref[pl.ds(pl.multiple_of(8 * group, 8), 8), :]
@@ -216,7 +214,7 @@
         rows = []
         for part in (edge, more):
             turned = pltpu.roll(part, 64, 1)
-            rows.append((jnp.where(first, part, turned), jnp.where(first, turned, part)))
+            rows.append((jnp.where(even, part, turned), jnp.where(even, turned, part)))
         coef_v = coef_ref[0, pl.ds(0, 8), :]
         made = []
         for p in range(PAIRS):
@@ -432,8 +430,11 @@
 def shards(fields, modes, pair_list, pair_value, assign):
     groups = lax.axis_size("term")
     count = lax.axis_size("space")
-    passes = []
+    passes, between = [], []
     for c in range(groups // 4):
+        for s in range(count):
+            one, two = ((holder(r, c) ^ mask_at(s)) * count + s for r in (1, 2))
+            between += [(one, two), (two, one)]
         for s in range(count - 1):
             lower = (holder(0, c) ^ mask_at(s + 1)) * count + s + 1
             upper = (holder(3, c) ^ mask_at(s)) * count + s
@@ -448,7 +449,7 @@
     edge = jnp.where(row_group(place) == 0, modes[:, 0], modes[:, modes.shape[1] - 1])
     coef = coefs(modes, lax.ppermute(edge, ("term", "space"), passes), weights)
     got, coef, places, own = lax.optimization_barrier((got, coef, places, own))
-    beyond = lax.ppermute(edges(got), ("term", "space"), passes)
+    beyond = lax.ppermute(edges(got), ("term", "space"), passes + between)
     diff, total = load(own, got, coef)
     mixed = mix(places, own, weights, diff, total, beyond, coef)
     back = lax.all_to_all(mixed, "term", 0, 0, axis_index_groups=[order], tiled=True)

time: 63.7 us -> 62.5 us (0.981)
  waiting for transfers between devices: 14.5 us -> 13.1 us
    all_to_all x1, waiting for transfers between devices: 9.9 us -> 8.52 us  [shards(): lax.all_to_all(sent, 'term', 0, 0, axis_index_groups=[order], tiled=True)]
where the time goes in v5:
time: 62.5 us; the launch traced here: 62.3 us
  blocking collectives  19.8 us (32%)
  starting transfers between devices  14.5 us (23%)
  waiting for transfers between devices  13.1 us (21%)
  Pallas kernels  7.68 us (12%)
  matrix products  3.15 us (5%)
  local copies, waits for them, and re-layouts  2.82 us (5%)
  other arithmetic  0.96 us (2%)
    all_to_all x1, blocking collectives, shards(): lax.all_to_all(mixed, 'term', 0, 0, axis_index_groups=[order], tiled=True)  19.8 us
    all_to_all x1, starting transfers between devices, shards(): lax.all_to_all(sent, 'term', 0, 0, axis_index_groups=[order], tiled=True)  8.95 us
    all_to_all x1, waiting for transfers between devices, shards(): lax.all_to_all(sent, 'term', 0, 0, axis_index_groups=[order], tiled=True)  8.52 us
    ppermute x1, waiting for transfers between devices, shards(): beyond = lax.ppermute(edges(got), ('term', 'space'), passes + between)  4.6 us
    ppermute x1, starting transfers between devices, shards(): coef = coefs(modes, lax.ppermute(edge, ('term', 'space'), passes), weights)  3.64 us
    dot_general x1, matrix products, tables(): lax.dot_general(at.astype(jnp.float32), value, (((0,), (0,)), ((), ())),...  3.15 us
    pallas_call x1, Pallas kernels, mix(): pl.pallas_call(mix_kernel, out_shape=f32(slots // (2 * PAIRS), BLOCK, 128...  2.66 us
    pallas_call x1, Pallas kernels, load(): pl.pallas_call(load_kernel, out_shape=(f32(slots, 16, 128), f32(slots, 8,...  2.15 us
  transfers between devices with their start and end apart: 3, of which 2 were waited for; matrix products, arithmetic and copies ran while one was open for 9% of the time, Pallas kernels for 4%

profile of v5, /device:TPU:16, one launch (start us, length us, event | category | flops | bytes accessed | tf_op | source)
XLA Modules:
  0.0 62.3 jit_solution(5137696212100592068)
XLA Ops:
  0.0 1.1 %copy-done.1 = f32[18,32,256]{2,1,0:T(8,128)S(1)} copy-done((f32[18,32,256]{2,1,0:T(8,128)S(1)}, f32[18,32,256]{2,1,0:T(8,128)}, u32[]{:S(2)}) %copy-start.1) | copy-done | bytes 589848
  1.1 1.7 %shard_map.64 = f32[16,88,128]{2,1,0:T(8,128)} custom-call(f32[18,32,256]{2,1,0:T(8,128)S(1)} %copy-done.1), custom_call_target="tpu_custom_call" | custom-call | bytes 6000000 | tf_op jit(solution)/shard_map/pallas_call | solution.py:324
  2.8 8.9 %all-to-all-start = ((f32[16,88,128]{2,1,0:T(8,128)}), f32[16,88,128]{2,1,0:T(8,128)S(1)}, u32[]{:S(2)}, u32[]{:S(2)}) async-start(f32[16,88,128]{2,1,0:T(8,128)} %shard_map.64), calls=%async_computation | async-start | bytes 1441792 | tf_op jit(solution)/shard_map/all_to_all | solution.py:446
  11.8 0.2 copy.14
  12.0 3.6 %collective-permute-start = (f32[11,256]{1,0:T(8,128)S(1)}, f32[11,256]{1,0:T(8,128)S(1)}, u32[]{:S(2)}, u32[]{:S(2)}) collective-permute-start(f32[11,256]{1,0:T(8,128)S(1)} %fusion.18), channel_id=1, source_target_pairs={{49,48},{48,49},{130,1},{1,130},{179,178},{178,179},{4,131},{131,4... | collective-permute-start | bytes 33800 | tf_op jit(solution)/shard_map/ppermute | solution.py:450
  15.8 0.6 gather_fusion
  16.4 0.1 eq.78
  16.5 0.3 select_reduce_fusion
  17.0 3.2 %fusion = f32[288,31]{0,1:T(8,128)S(1)} fusion(s32[2048]{0:T(1024)S(1)} %bitcast.7, f32[2048]{0:T(1024)S(1)} %convert_element_type.14, f32[2048]{0:T(1024)S(1)} %copy-done.5, s32[31]{0:T(128)S(1)} %iota_select_fusion, s32[2048]{0:T(1024)S(1)} %bitcast.6, pred[2048]{0:T(1024)(128)(4,1)S(1)} %get-tuple-element.22, pred[31]{0:T(512)(128)(4,1)S(1)} %get-tuple-element.28, ...), kind=kOutput, calls=%fused_computation.2 | convolution fusion | flops 220385280 | bytes 74810 | tf_op jit(solution)/shard_map/dot_general | solution.py:413
  20.1 0.1 copy.18
  20.2 0.1 reshape.52
  20.4 0.1 iota_compare_fusion.2
  20.6 0.2 select_reduce_fusion.1
  20.9 0.1 copy.20
  21.0 0.3 broadcast_in_dim.145.weight_ref
  21.3 0.2 shard_map.65.coef_ref
  21.5 8.5 %all-to-all-done.got_ref = f32[16,88,128]{2,1,0:T(8,128)S(1)} async-done(((f32[16,88,128]{2,1,0:T(8,128)}), f32[16,88,128]{2,1,0:T(8,128)S(1)}, u32[]{:S(2)}, u32[]{:S(2)}) %all-to-all-start) | async-done | bytes 720928 | tf_op jit(solution)/shard_map/all_to_all | solution.py:446
  30.0 0.1 broadcast_in_dim.151.own_ref
  30.2 1.9 %collective-permute-start.1 = (f32[144,128]{1,0:T(8,128)S(1)}, f32[144,128]{1,0:T(8,128)S(1)}, u32[]{:S(2)}, u32[]{:S(2)}) collective-permute-start(f32[144,128]{1,0:T(8,128)S(1)} %shard_map.67), channel_id=1, source_target_pairs={{49,48},{48,49},{130,1},{1,130},{179,178},{178,179},{4,131},{131,4... | collective-permute-start | bytes 221192 | tf_op jit(solution)/shard_map/ppermute | solution.py:452
  32.1 2.1 %shard_map.66 = (f32[288,16,128]{2,1,0:T(8,128)S(1)}, f32[288,8,128]{2,1,0:T(8,128)S(1)}) custom-call(f32[288,128]{1,0:T(8,128)S(1)} %broadcast_in_dim.151.own_ref, f32[16,88,128]{2,1,0:T(8,128)S(1)} %all-to-all-done.got_ref, f32[11,16,128]{2,1,0:T(8,128)S(1)} %shard_map.65.coef_ref), custom_call_target="tpu_custom_call" | custom-call | bytes 12000000 | tf_op jit(solution)/shard_map/pallas_call | solution.py:362
  34.3 4.6 %collective-permute-done.1.edge_ref = f32[144,128]{1,0:T(8,128)S(1)} collective-permute-done((f32[144,128]{1,0:T(8,128)S(1)}, f32[144,128]{1,0:T(8,128)S(1)}, u32[]{:S(2)}, u32[]{:S(2)}) %collective-permute-start.1) | collective-permute-done | bytes 73760 | tf_op jit(solution)/shard_map/ppermute | solution.py:452
  38.9 2.7 %shard_map.68 = f32[16,72,128]{2,1,0:T(8,128)S(1)} custom-call(s32[1024]{0:T(1024)S(1)} %pad.9.place_ref, f32[288,128]{1,0:T(8,128)S(1)} %broadcast_in_dim.151.own_ref, f32[66,24,128]{2,1,0:T(8,128)S(1)} %broadcast_in_dim.145.weight_ref, f32[288,16,128]{2,1,0:T(8,128)S(1)} %get-tuple-element.19.diff_ref, f32[288,8,128]{2,1,0:T(8,128)S(1)} %get-tuple-element.20.start_ref, ...), custom_call_target="tpu_custom_call" | custom-call | bytes 15000000 | tf_op jit(solution)/shard_map/pallas_call | solution.py:374
  41.5 19.8 %all_to_all.10.got_ref = f32[16,72,128]{2,1,0:T(8,128)S(1)} all-to-all(f32[16,72,128]{2,1,0:T(8,128)S(1)} %shard_map.68), channel_id=1, replica_groups={{128,0,192,64,160,32,224,96,144,16,208,80,176,48,240,112},{129,1,193,65..., dimensions={0} | all-to-all | bytes 1179648 | tf_op jit(solution)/shard_map/all_to_all | solution.py:455
  61.3 0.9 %shard_map.69 = f32[18,32,256]{2,1,0:T(8,128)} custom-call(f32[16,72,128]{2,1,0:T(8,128)S(1)} %all_to_all.10.got_ref), custom_call_target="tpu_custom_call" | custom-call | bytes 3000000 | tf_op jit(solution)/shard_map/pallas_call | solution.py:391
  (28 shorter events, 0.5 us)
Async XLA Ops:
  0.0 15.8 %copy-start.4 = (s32[16]{0:T(128)S(1)}, s32[16]{0:T(128)}, u32[]{:S(2)}) copy-start(s32[16]{0:T(128)} %constant.52) | copy-start | bytes 196
  0.0 11.8 %copy-start = (f32[11,32,256]{2,1,0:T(8,128)S(1)}, f32[11,32,256]{2,1,0:T(8,128)}, u32[]{:S(2)}) copy-start(f32[11,32,256]{2,1,0:T(8,128)} %modes_ref) | copy-start | bytes 1081348
  0.0 1.1 %copy-start.1 = (f32[18,32,256]{2,1,0:T(8,128)S(1)}, f32[18,32,256]{2,1,0:T(8,128)}, u32[]{:S(2)}) copy-start(f32[18,32,256]{2,1,0:T(8,128)} %f_ref.1) | copy-start | bytes 1769476
  1.1 14.6 %copy-start.2 = (s32[2048,3]{0,1:T(4,128)S(1)}, s32[2048,3]{0,1:T(4,128)}, u32[]{:S(2)}) copy-start(s32[2048,3]{0,1:T(4,128)} %param.8) | copy-start | bytes 73732
  1.1 14.6 %copy-start.3 = (s32[288]{0:T(512)S(1)}, s32[288]{0:T(512)}, u32[]{:S(2)}) copy-start(s32[288]{0:T(512)} %param.10) | copy-start | bytes 3460
  1.1 15.8 %copy-start.5 = (f32[2048]{0:T(1024)S(1)}, f32[2048]{0:T(1024)}, u32[]{:S(2)}) copy-start(f32[2048]{0:T(1024)} %param.9) | copy-start | bytes 24580
  2.8 27.2 %all-to-all-start = ((f32[16,88,128]{2,1,0:T(8,128)}), f32[16,88,128]{2,1,0:T(8,128)S(1)}, u32[]{:S(2)}, u32[]{:S(2)}) async-start(f32[16,88,128]{2,1,0:T(8,128)} %shard_map.64), calls=%async_computation | async-start | bytes 1441792 | tf_op jit(solution)/shard_map/all_to_all | solution.py:446
  12.0 9.0 %collective-permute-start = (f32[11,256]{1,0:T(8,128)S(1)}, f32[11,256]{1,0:T(8,128)S(1)}, u32[]{:S(2)}, u32[]{:S(2)}) collective-permute-start(f32[11,256]{1,0:T(8,128)S(1)} %fusion.18), channel_id=1, source_target_pairs={{49,48},{48,49},{130,1},{1,130},{179,178},{178,179},{4,131},{131,4... | collective-permute-start | bytes 33800 | tf_op jit(solution)/shard_map/ppermute | solution.py:450
  30.2 8.7 %collective-permute-start.1 = (f32[144,128]{1,0:T(8,128)S(1)}, f32[144,128]{1,0:T(8,128)S(1)}, u32[]{:S(2)}, u32[]{:S(2)}) collective-permute-start(f32[144,128]{1,0:T(8,128)S(1)} %shard_map.67), channel_id=1, source_target_pairs={{49,48},{48,49},{130,1},{1,130},{179,178},{178,179},{4,131},{131,4... | collective-permute-start | bytes 221192 | tf_op jit(solution)/shard_map/ppermute | solution.py:452

commit v6 on v5

--- a/solution.py
+++ b/solution.py
@@ -19,6 +19,7 @@
 
 
 def rank(device):
+    device = device ^ 15
     return (device & 1) << 3 | (device & 2) << 1 | (device & 4) >> 1 | (device >> 3 ^ 1)
 
 

time: 62.5 us -> 61.8 us (0.989)
  waiting for transfers between devices: 13.1 us -> 10.2 us
  starting transfers between devices: 14.5 us -> 16.9 us
    all_to_all x1, waiting for transfers between devices: 8.52 us -> 5.38 us  [shards(): lax.all_to_all(sent, 'term', 0, 0, axis_index_groups=[order], tiled=True)]
    ppermute x1, waiting for transfers between devices: 0.01 us -> 1.32 us  [shards(): coef = coefs(modes, lax.ppermute(edge, ('term', 'space'), passes), weights)]
    ppermute x1, waiting for transfers between devices: 4.6 us -> 3.55 us  [shards(): beyond = lax.ppermute(edges(got), ('term', 'space'), passes + between)]
    ppermute x1, starting transfers between devices: 1.92 us -> 2.96 us  [shards(): beyond = lax.ppermute(edges(got), ('term', 'space'), passes + between)]
    ppermute x1, starting transfers between devices: 3.64 us -> 4.44 us  [shards(): coef = coefs(modes, lax.ppermute(edge, ('term', 'space'), passes), weights)]
  transfers between devices with their start and end apart: 3 -> 3, of which waited for: 2 -> 3; matrix products, arithmetic and copies ran while one was open for 9% -> 9% of each run, Pallas kernels for 4% -> 4%
where the time goes in v6:
time: 61.8 us; the launch traced here: 61.5 us
  blocking collectives  19.5 us (32%)
  starting transfers between devices  16.9 us (27%)
  waiting for transfers between devices  10.2 us (17%)
  Pallas kernels  7.68 us (12%)
  matrix products  3.15 us (5%)
  local copies, waits for them, and re-layouts  2.82 us (5%)
  other arithmetic  0.96 us (2%)
    all_to_all x1, blocking collectives, shards(): lax.all_to_all(mixed, 'term', 0, 0, axis_index_groups=[order], tiled=True)  19.5 us
    all_to_all x1, starting transfers between devices, shards(): lax.all_to_all(sent, 'term', 0, 0, axis_index_groups=[order], tiled=True)  9.53 us
    all_to_all x1, waiting for transfers between devices, shards(): lax.all_to_all(sent, 'term', 0, 0, axis_index_groups=[order], tiled=True)  5.38 us
    ppermute x1, starting transfers between devices, shards(): coef = coefs(modes, lax.ppermute(edge, ('term', 'space'), passes), weights)  4.44 us
    ppermute x1, waiting for transfers between devices, shards(): beyond = lax.ppermute(edges(got), ('term', 'space'), passes + between)  3.55 us
    dot_general x1, matrix products, tables(): lax.dot_general(at.astype(jnp.float32), value, (((0,), (0,)), ((), ())),...  3.15 us
    ppermute x1, starting transfers between devices, shards(): beyond = lax.ppermute(edges(got), ('term', 'space'), passes + between)  2.96 us
    pallas_call x1, Pallas kernels, mix(): pl.pallas_call(mix_kernel, out_shape=f32(slots // (2 * PAIRS), BLOCK, 128...  2.65 us
  transfers between devices with their start and end apart: 3, of which 3 were waited for; matrix products, arithmetic and copies ran while one was open for 9% of the time, Pallas kernels for 4%

profile of v6, /device:TPU:16, one launch (start us, length us, event | category | flops | bytes accessed | tf_op | source)
XLA Modules:
  0.0 61.5 jit_solution(16689905593622014209)
XLA Ops:
  0.0 1.1 %copy-done.1 = f32[18,32,256]{2,1,0:T(8,128)S(1)} copy-done((f32[18,32,256]{2,1,0:T(8,128)S(1)}, f32[18,32,256]{2,1,0:T(8,128)}, u32[]{:S(2)}) %copy-start.1) | copy-done | bytes 589848
  1.1 1.7 %shard_map.64 = f32[16,88,128]{2,1,0:T(8,128)} custom-call(f32[18,32,256]{2,1,0:T(8,128)S(1)} %copy-done.1), custom_call_target="tpu_custom_call" | custom-call | bytes 6000000 | tf_op jit(solution)/shard_map/pallas_call | solution.py:325
  2.8 9.5 %all-to-all-start = ((f32[16,88,128]{2,1,0:T(8,128)}), f32[16,88,128]{2,1,0:T(8,128)S(1)}, u32[]{:S(2)}, u32[]{:S(2)}) async-start(f32[16,88,128]{2,1,0:T(8,128)} %shard_map.64), calls=%async_computation | async-start | bytes 1441792 | tf_op jit(solution)/shard_map/all_to_all | solution.py:447
  12.4 0.2 copy.14
  12.6 4.4 %collective-permute-start = (f32[11,256]{1,0:T(8,128)S(1)}, f32[11,256]{1,0:T(8,128)S(1)}, u32[]{:S(2)}, u32[]{:S(2)}) collective-permute-start(f32[11,256]{1,0:T(8,128)S(1)} %fusion.18), channel_id=1, source_target_pairs={{49,48},{48,49},{130,1},{1,130},{179,178},{178,179},{4,131},{131,4... | collective-permute-start | bytes 33800 | tf_op jit(solution)/shard_map/ppermute | solution.py:451
  17.2 0.6 gather_fusion
  17.9 0.3 select_reduce_fusion
  18.3 3.2 %fusion = f32[288,31]{0,1:T(8,128)S(1)} fusion(s32[2048]{0:T(1024)S(1)} %bitcast.7, f32[2048]{0:T(1024)S(1)} %convert_element_type.14, f32[2048]{0:T(1024)S(1)} %copy-done.5, s32[31]{0:T(128)S(1)} %iota_select_fusion, s32[2048]{0:T(1024)S(1)} %bitcast.6, pred[2048]{0:T(1024)(128)(4,1)S(1)} %get-tuple-element.22, pred[31]{0:T(512)(128)(4,1)S(1)} %get-tuple-element.28, ...), kind=kOutput, calls=%fused_computation.2 | convolution fusion | flops 220385280 | bytes 74810 | tf_op jit(solution)/shard_map/dot_general | solution.py:414
  21.5 0.1 copy.18
  21.6 0.1 reshape.52
  21.8 0.1 iota_compare_fusion.2
  22.0 0.2 select_reduce_fusion.1
  22.3 0.1 copy.20
  22.4 1.3 %collective-permute-done.edge_ref = f32[11,256]{1,0:T(8,128)S(1)} collective-permute-done((f32[11,256]{1,0:T(8,128)S(1)}, f32[11,256]{1,0:T(8,128)S(1)}, u32[]{:S(2)}, u32[]{:S(2)}) %collective-permute-start) | collective-permute-done | bytes 11296 | tf_op jit(solution)/shard_map/ppermute | solution.py:451
  23.7 0.3 broadcast_in_dim.145.weight_ref
  24.0 0.2 shard_map.65.coef_ref
  24.2 5.4 %all-to-all-done.got_ref = f32[16,88,128]{2,1,0:T(8,128)S(1)} async-done(((f32[16,88,128]{2,1,0:T(8,128)}), f32[16,88,128]{2,1,0:T(8,128)S(1)}, u32[]{:S(2)}, u32[]{:S(2)}) %all-to-all-start) | async-done | bytes 720928 | tf_op jit(solution)/shard_map/all_to_all | solution.py:447
  29.6 0.1 broadcast_in_dim.151.own_ref
  29.7 3.0 %collective-permute-start.1 = (f32[144,128]{1,0:T(8,128)S(1)}, f32[144,128]{1,0:T(8,128)S(1)}, u32[]{:S(2)}, u32[]{:S(2)}) collective-permute-start(f32[144,128]{1,0:T(8,128)S(1)} %shard_map.67), channel_id=1, source_target_pairs={{49,48},{48,49},{130,1},{1,130},{179,178},{178,179},{4,131},{131,4... | collective-permute-start | bytes 221192 | tf_op jit(solution)/shard_map/ppermute | solution.py:453
  32.7 2.1 %shard_map.66 = (f32[288,16,128]{2,1,0:T(8,128)S(1)}, f32[288,8,128]{2,1,0:T(8,128)S(1)}) custom-call(f32[288,128]{1,0:T(8,128)S(1)} %broadcast_in_dim.151.own_ref, f32[16,88,128]{2,1,0:T(8,128)S(1)} %all-to-all-done.got_ref, f32[11,16,128]{2,1,0:T(8,128)S(1)} %shard_map.65.coef_ref), custom_call_target="tpu_custom_call" | custom-call | bytes 12000000 | tf_op jit(solution)/shard_map/pallas_call | solution.py:363
  34.9 3.6 %collective-permute-done.1.edge_ref = f32[144,128]{1,0:T(8,128)S(1)} collective-permute-done((f32[144,128]{1,0:T(8,128)S(1)}, f32[144,128]{1,0:T(8,128)S(1)}, u32[]{:S(2)}, u32[]{:S(2)}) %collective-permute-start.1) | collective-permute-done | bytes 73760 | tf_op jit(solution)/shard_map/ppermute | solution.py:453
  38.4 2.7 %shard_map.68 = f32[16,72,128]{2,1,0:T(8,128)S(1)} custom-call(s32[1024]{0:T(1024)S(1)} %pad.9.place_ref, f32[288,128]{1,0:T(8,128)S(1)} %broadcast_in_dim.151.own_ref, f32[66,24,128]{2,1,0:T(8,128)S(1)} %broadcast_in_dim.145.weight_ref, f32[288,16,128]{2,1,0:T(8,128)S(1)} %get-tuple-element.19.diff_ref, f32[288,8,128]{2,1,0:T(8,128)S(1)} %get-tuple-element.20.start_ref, ...), custom_call_target="tpu_custom_call" | custom-call | bytes 15000000 | tf_op jit(solution)/shard_map/pallas_call | solution.py:375
  41.1 19.5 %all_to_all.10.got_ref = f32[16,72,128]{2,1,0:T(8,128)S(1)} all-to-all(f32[16,72,128]{2,1,0:T(8,128)S(1)} %shard_map.68), channel_id=1, replica_groups={{112,240,48,176,80,208,16,144,96,224,32,160,64,192,0,128},{113,241,49,1..., dimensions={0} | all-to-all | bytes 1179648 | tf_op jit(solution)/shard_map/all_to_all | solution.py:456
  60.6 1.0 %shard_map.69 = f32[18,32,256]{2,1,0:T(8,128)} custom-call(f32[16,72,128]{2,1,0:T(8,128)S(1)} %all_to_all.10.got_ref), custom_call_target="tpu_custom_call" | custom-call | bytes 3000000 | tf_op jit(solution)/shard_map/pallas_call | solution.py:392
  (28 shorter events, 0.5 us)
Async XLA Ops:
  0.0 17.2 %copy-start.4 = (s32[16]{0:T(128)S(1)}, s32[16]{0:T(128)}, u32[]{:S(2)}) copy-start(s32[16]{0:T(128)} %constant.52) | copy-start | bytes 196
  0.0 12.4 %copy-start = (f32[11,32,256]{2,1,0:T(8,128)S(1)}, f32[11,32,256]{2,1,0:T(8,128)}, u32[]{:S(2)}) copy-start(f32[11,32,256]{2,1,0:T(8,128)} %modes_ref) | copy-start | bytes 1081348
  0.0 1.1 %copy-start.1 = (f32[18,32,256]{2,1,0:T(8,128)S(1)}, f32[18,32,256]{2,1,0:T(8,128)}, u32[]{:S(2)}) copy-start(f32[18,32,256]{2,1,0:T(8,128)} %f_ref.1) | copy-start | bytes 1769476
  1.1 16.0 %copy-start.2 = (s32[2048,3]{0,1:T(4,128)S(1)}, s32[2048,3]{0,1:T(4,128)}, u32[]{:S(2)}) copy-start(s32[2048,3]{0,1:T(4,128)} %param.8) | copy-start | bytes 73732
  1.1 16.0 %copy-start.3 = (s32[288]{0:T(512)S(1)}, s32[288]{0:T(512)}, u32[]{:S(2)}) copy-start(s32[288]{0:T(512)} %param.10) | copy-start | bytes 3460
  1.1 17.2 %copy-start.5 = (f32[2048]{0:T(1024)S(1)}, f32[2048]{0:T(1024)}, u32[]{:S(2)}) copy-start(f32[2048]{0:T(1024)} %param.9) | copy-start | bytes 24580
  2.8 26.8 %all-to-all-start = ((f32[16,88,128]{2,1,0:T(8,128)}), f32[16,88,128]{2,1,0:T(8,128)S(1)}, u32[]{:S(2)}, u32[]{:S(2)}) async-start(f32[16,88,128]{2,1,0:T(8,128)} %shard_map.64), calls=%async_computation | async-start | bytes 1441792 | tf_op jit(solution)/shard_map/all_to_all | solution.py:447
  12.6 11.1 %collective-permute-start = (f32[11,256]{1,0:T(8,128)S(1)}, f32[11,256]{1,0:T(8,128)S(1)}, u32[]{:S(2)}, u32[]{:S(2)}) collective-permute-start(f32[11,256]{1,0:T(8,128)S(1)} %fusion.18), channel_id=1, source_target_pairs={{49,48},{48,49},{130,1},{1,130},{179,178},{178,179},{4,131},{131,4... | collective-permute-start | bytes 33800 | tf_op jit(solution)/shard_map/ppermute | solution.py:451
  29.7 8.7 %collective-permute-start.1 = (f32[144,128]{1,0:T(8,128)S(1)}, f32[144,128]{1,0:T(8,128)S(1)}, u32[]{:S(2)}, u32[]{:S(2)}) collective-permute-start(f32[144,128]{1,0:T(8,128)S(1)} %shard_map.67), channel_id=1, source_target_pairs={{49,48},{48,49},{130,1},{1,130},{179,178},{178,179},{4,131},{131,4... | collective-permute-start | bytes 221192 | tf_op jit(solution)/shard_map/ppermute | solution.py:453

commit v7 on v6

--- a/solution.py
+++ b/solution.py
@@ -228,7 +228,7 @@
         for slot, vert, hori, value in made:
             diff[slot, pl.ds(0, 8), :] = vert
             diff[slot, pl.ds(8, 8), :] = hori
-            total[slot] = value
+            total[slot, pl.ds(0, 8), :] = value
         return carry
 
     lax.fori_loop(0, groups, patch, 0, unroll=4)
@@ -257,25 +257,25 @@
             mine.append(parts[0])
         for i, term in enumerate(terms):
             lower = places[term]
-            total[lower] = total[lower] + mine[i]
-            sums = [total[uppers[i * VARS + v]] + gains[i * VARS + v] for v in range(VARS)]
+            total[lower, pl.ds(0, 8), :] = total[lower, pl.ds(0, 8), :] + mine[i]
+            sums = [total[uppers[i * VARS + v], pl.ds(0, 8), :] + gains[i * VARS + v] for v in range(VARS)]
             for v in range(VARS):
-                total[uppers[i * VARS + v]] = sums[v]
+                total[uppers[i * VARS + v], pl.ds(0, 8), :] = sums[v]
         return carry
 
-    lax.fori_loop(0, LOWER // 6, couple, 0)
+    lax.fori_loop(0, LOWER // 6, couple, 0, unroll=2)
 
     def store(group, carry):
         made = []
         for p in range(PAIRS):
-            a = total[group * (2 * PAIRS) + p]
-            b = total[group * (2 * PAIRS) + PAIRS + p]
+            a = total[group * (2 * PAIRS) + p, pl.ds(0, 8), :]
+            b = total[group * (2 * PAIRS) + PAIRS + p, pl.ds(0, 8), :]
             made.append(jnp.where(low, a, b) + pltpu.roll(jnp.where(low, b, a), 64, 1))
         for p in range(PAIRS):
             out_ref[group, pl.ds(8 * p, 8), :] = made[p]
         return carry
 
-    lax.fori_loop(0, groups, store, 0, unroll=8)
+    lax.fori_loop(0, groups, store, 0, unroll=16)
 
 
 def unpack_kernel(got_ref, result_ref, out_ref, sem):
@@ -379,7 +379,7 @@
         out_specs=vmem(),
         scratch_shapes=[
             pltpu.VMEM((slots, 16, 128), jnp.float32),
-            pltpu.VMEM((slots, 8, 128), jnp.float32),
+            pltpu.VMEM((slots, 16, 128), jnp.float32),
             pltpu.SMEM(places.shape, jnp.int32),
             pltpu.SemaphoreType.DMA,
         ],

time: 61.8 us -> 61.6 us (level)
  no operation moved by 1% of the time
where the time goes in v7:
time: 61.6 us; the launch traced here: 61.3 us
  blocking collectives  19.5 us (32%)
  starting transfers between devices  16.9 us (27%)
  waiting for transfers between devices  10.2 us (17%)
  Pallas kernels  7.49 us (12%)
  matrix products  3.15 us (5%)
  local copies, waits for them, and re-layouts  2.82 us (5%)
  other arithmetic  0.96 us (2%)
    all_to_all x1, blocking collectives, shards(): lax.all_to_all(mixed, 'term', 0, 0, axis_index_groups=[order], tiled=True)  19.5 us
    all_to_all x1, starting transfers between devices, shards(): lax.all_to_all(sent, 'term', 0, 0, axis_index_groups=[order], tiled=True)  9.53 us
    all_to_all x1, waiting for transfers between devices, shards(): lax.all_to_all(sent, 'term', 0, 0, axis_index_groups=[order], tiled=True)  5.38 us
    ppermute x1, starting transfers between devices, shards(): coef = coefs(modes, lax.ppermute(edge, ('term', 'space'), passes), weights)  4.44 us
    ppermute x1, waiting for transfers between devices, shards(): beyond = lax.ppermute(edges(got), ('term', 'space'), passes + between)  3.55 us
    dot_general x1, matrix products, tables(): lax.dot_general(at.astype(jnp.float32), value, (((0,), (0,)), ((), ())),...  3.15 us
    ppermute x1, starting transfers between devices, shards(): beyond = lax.ppermute(edges(got), ('term', 'space'), passes + between)  2.96 us
    pallas_call x1, Pallas kernels, mix(): pl.pallas_call(mix_kernel, out_shape=f32(slots // (2 * PAIRS), BLOCK, 128...  2.45 us
  transfers between devices with their start and end apart: 3, of which 3 were waited for; matrix products, arithmetic and copies ran while one was open for 9% of the time, Pallas kernels for 4%

profile of v7, /device:TPU:16, one launch (start us, length us, event | category | flops | bytes accessed | tf_op | source)
XLA Modules:
  0.0 61.3 jit_solution(18244548325067841971)
XLA Ops:
  0.0 1.1 %copy-done.1 = f32[18,32,256]{2,1,0:T(8,128)S(1)} copy-done((f32[18,32,256]{2,1,0:T(8,128)S(1)}, f32[18,32,256]{2,1,0:T(8,128)}, u32[]{:S(2)}) %copy-start.1) | copy-done | bytes 589848
  1.1 1.7 %shard_map.64 = f32[16,88,128]{2,1,0:T(8,128)} custom-call(f32[18,32,256]{2,1,0:T(8,128)S(1)} %copy-done.1), custom_call_target="tpu_custom_call" | custom-call | bytes 6000000 | tf_op jit(solution)/shard_map/pallas_call | solution.py:325
  2.8 9.5 %all-to-all-start = ((f32[16,88,128]{2,1,0:T(8,128)}), f32[16,88,128]{2,1,0:T(8,128)S(1)}, u32[]{:S(2)}, u32[]{:S(2)}) async-start(f32[16,88,128]{2,1,0:T(8,128)} %shard_map.64), calls=%async_computation | async-start | bytes 1441792 | tf_op jit(solution)/shard_map/all_to_all | solution.py:447
  12.4 0.2 copy.14
  12.6 4.4 %collective-permute-start = (f32[11,256]{1,0:T(8,128)S(1)}, f32[11,256]{1,0:T(8,128)S(1)}, u32[]{:S(2)}, u32[]{:S(2)}) collective-permute-start(f32[11,256]{1,0:T(8,128)S(1)} %fusion.18), channel_id=1, source_target_pairs={{49,48},{48,49},{130,1},{1,130},{179,178},{178,179},{4,131},{131,4... | collective-permute-start | bytes 33800 | tf_op jit(solution)/shard_map/ppermute | solution.py:451
  17.2 0.6 gather_fusion
  17.9 0.3 select_reduce_fusion
  18.3 3.2 %fusion = f32[288,31]{0,1:T(8,128)S(1)} fusion(s32[2048]{0:T(1024)S(1)} %bitcast.7, f32[2048]{0:T(1024)S(1)} %convert_element_type.14, f32[2048]{0:T(1024)S(1)} %copy-done.5, s32[31]{0:T(128)S(1)} %iota_select_fusion, s32[2048]{0:T(1024)S(1)} %bitcast.6, pred[2048]{0:T(1024)(128)(4,1)S(1)} %get-tuple-element.22, pred[31]{0:T(512)(128)(4,1)S(1)} %get-tuple-element.28, ...), kind=kOutput, calls=%fused_computation.2 | convolution fusion | flops 220385280 | bytes 74810 | tf_op jit(solution)/shard_map/dot_general | solution.py:414
  21.5 0.1 copy.18
  21.6 0.1 reshape.52
  21.8 0.1 iota_compare_fusion.2
  22.0 0.2 select_reduce_fusion.1
  22.3 0.1 copy.20
  22.4 1.3 %collective-permute-done.edge_ref = f32[11,256]{1,0:T(8,128)S(1)} collective-permute-done((f32[11,256]{1,0:T(8,128)S(1)}, f32[11,256]{1,0:T(8,128)S(1)}, u32[]{:S(2)}, u32[]{:S(2)}) %collective-permute-start) | collective-permute-done | bytes 11296 | tf_op jit(solution)/shard_map/ppermute | solution.py:451
  23.7 0.3 broadcast_in_dim.145.weight_ref
  24.0 0.2 shard_map.65.coef_ref
  24.2 5.4 %all-to-all-done.got_ref = f32[16,88,128]{2,1,0:T(8,128)S(1)} async-done(((f32[16,88,128]{2,1,0:T(8,128)}), f32[16,88,128]{2,1,0:T(8,128)S(1)}, u32[]{:S(2)}, u32[]{:S(2)}) %all-to-all-start) | async-done | bytes 720928 | tf_op jit(solution)/shard_map/all_to_all | solution.py:447
  29.6 0.1 broadcast_in_dim.151.own_ref
  29.7 3.0 %collective-permute-start.1 = (f32[144,128]{1,0:T(8,128)S(1)}, f32[144,128]{1,0:T(8,128)S(1)}, u32[]{:S(2)}, u32[]{:S(2)}) collective-permute-start(f32[144,128]{1,0:T(8,128)S(1)} %shard_map.67), channel_id=1, source_target_pairs={{49,48},{48,49},{130,1},{1,130},{179,178},{178,179},{4,131},{131,4... | collective-permute-start | bytes 221192 | tf_op jit(solution)/shard_map/ppermute | solution.py:453
  32.7 2.1 %shard_map.66 = (f32[288,16,128]{2,1,0:T(8,128)S(1)}, f32[288,8,128]{2,1,0:T(8,128)S(1)}) custom-call(f32[288,128]{1,0:T(8,128)S(1)} %broadcast_in_dim.151.own_ref, f32[16,88,128]{2,1,0:T(8,128)S(1)} %all-to-all-done.got_ref, f32[11,16,128]{2,1,0:T(8,128)S(1)} %shard_map.65.coef_ref), custom_call_target="tpu_custom_call" | custom-call | bytes 12000000 | tf_op jit(solution)/shard_map/pallas_call | solution.py:363
  34.9 3.6 %collective-permute-done.1.edge_ref = f32[144,128]{1,0:T(8,128)S(1)} collective-permute-done((f32[144,128]{1,0:T(8,128)S(1)}, f32[144,128]{1,0:T(8,128)S(1)}, u32[]{:S(2)}, u32[]{:S(2)}) %collective-permute-start.1) | collective-permute-done | bytes 73760 | tf_op jit(solution)/shard_map/ppermute | solution.py:453
  38.4 2.5 %shard_map.68 = f32[16,72,128]{2,1,0:T(8,128)S(1)} custom-call(s32[1024]{0:T(1024)S(1)} %pad.9.place_ref, f32[288,128]{1,0:T(8,128)S(1)} %broadcast_in_dim.151.own_ref, f32[66,24,128]{2,1,0:T(8,128)S(1)} %broadcast_in_dim.145.weight_ref, f32[288,16,128]{2,1,0:T(8,128)S(1)} %get-tuple-element.19.diff_ref, f32[288,8,128]{2,1,0:T(8,128)S(1)} %get-tuple-element.20.start_ref, ...), custom_call_target="tpu_custom_call" | custom-call | bytes 15000000 | tf_op jit(solution)/shard_map/pallas_call | solution.py:375
  40.9 19.5 %all_to_all.10.got_ref = f32[16,72,128]{2,1,0:T(8,128)S(1)} all-to-all(f32[16,72,128]{2,1,0:T(8,128)S(1)} %shard_map.68), channel_id=1, replica_groups={{112,240,48,176,80,208,16,144,96,224,32,160,64,192,0,128},{113,241,49,1..., dimensions={0} | all-to-all | bytes 1179648 | tf_op jit(solution)/shard_map/all_to_all | solution.py:456
  60.4 1.0 %shard_map.69 = f32[18,32,256]{2,1,0:T(8,128)} custom-call(f32[16,72,128]{2,1,0:T(8,128)S(1)} %all_to_all.10.got_ref), custom_call_target="tpu_custom_call" | custom-call | bytes 3000000 | tf_op jit(solution)/shard_map/pallas_call | solution.py:392
  (28 shorter events, 0.5 us)
Async XLA Ops:
  0.0 17.2 %copy-start.4 = (s32[16]{0:T(128)S(1)}, s32[16]{0:T(128)}, u32[]{:S(2)}) copy-start(s32[16]{0:T(128)} %constant.52) | copy-start | bytes 196
  0.0 12.4 %copy-start = (f32[11,32,256]{2,1,0:T(8,128)S(1)}, f32[11,32,256]{2,1,0:T(8,128)}, u32[]{:S(2)}) copy-start(f32[11,32,256]{2,1,0:T(8,128)} %modes_ref) | copy-start | bytes 1081348
  0.0 1.1 %copy-start.1 = (f32[18,32,256]{2,1,0:T(8,128)S(1)}, f32[18,32,256]{2,1,0:T(8,128)}, u32[]{:S(2)}) copy-start(f32[18,32,256]{2,1,0:T(8,128)} %f_ref.1) | copy-start | bytes 1769476
  1.1 16.0 %copy-start.2 = (s32[2048,3]{0,1:T(4,128)S(1)}, s32[2048,3]{0,1:T(4,128)}, u32[]{:S(2)}) copy-start(s32[2048,3]{0,1:T(4,128)} %param.8) | copy-start | bytes 73732
  1.1 16.0 %copy-start.3 = (s32[288]{0:T(512)S(1)}, s32[288]{0:T(512)}, u32[]{:S(2)}) copy-start(s32[288]{0:T(512)} %param.10) | copy-start | bytes 3460
  1.1 17.2 %copy-start.5 = (f32[2048]{0:T(1024)S(1)}, f32[2048]{0:T(1024)}, u32[]{:S(2)}) copy-start(f32[2048]{0:T(1024)} %param.9) | copy-start | bytes 24580
  2.8 26.8 %all-to-all-start = ((f32[16,88,128]{2,1,0:T(8,128)}), f32[16,88,128]{2,1,0:T(8,128)S(1)}, u32[]{:S(2)}, u32[]{:S(2)}) async-start(f32[16,88,128]{2,1,0:T(8,128)} %shard_map.64), calls=%async_computation | async-start | bytes 1441792 | tf_op jit(solution)/shard_map/all_to_all | solution.py:447
  12.6 11.1 %collective-permute-start = (f32[11,256]{1,0:T(8,128)S(1)}, f32[11,256]{1,0:T(8,128)S(1)}, u32[]{:S(2)}, u32[]{:S(2)}) collective-permute-start(f32[11,256]{1,0:T(8,128)S(1)} %fusion.18), channel_id=1, source_target_pairs={{49,48},{48,49},{130,1},{1,130},{179,178},{178,179},{4,131},{131,4... | collective-permute-start | bytes 33800 | tf_op jit(solution)/shard_map/ppermute | solution.py:451
  29.7 8.7 %collective-permute-start.1 = (f32[144,128]{1,0:T(8,128)S(1)}, f32[144,128]{1,0:T(8,128)S(1)}, u32[]{:S(2)}, u32[]{:S(2)}) collective-permute-start(f32[144,128]{1,0:T(8,128)S(1)} %shard_map.67), channel_id=1, source_target_pairs={{49,48},{48,49},{130,1},{1,130},{179,178},{178,179},{4,131},{131,4... | collective-permute-start | bytes 221192 | tf_op jit(solution)/shard_map/ppermute | solution.py:453

commit v8 on v7

--- a/solution.py
+++ b/solution.py
@@ -51,9 +51,12 @@
     spare = lane % 64 >= 32
     mask, _ = here()
 
-    def send(r, c):
+    def send(r, c, part):
         to = rank(holder(r, c) ^ mask)
-        return pltpu.make_async_copy(out_ref.at[to], sent_ref.at[to], out_sem.at[4 * r + c])
+        rows = pl.ds(0, BLOCK) if part == 0 else pl.ds(BLOCK, ROWS - BLOCK)
+        return pltpu.make_async_copy(
+            out_ref.at[to, rows], sent_ref.at[to, rows], out_sem.at[part, 4 * r + c]
+        )
 
     for r in range(4):
         near, far = [], []
@@ -91,13 +94,15 @@
             moved = pltpu.roll(pltpu.roll(sides[c], 32, 1), 2, 0)
             kept = jnp.where(spare, moved, sides[c])
             out_ref[rank(holder(r, c) ^ mask), pl.ds(SIDE, 7), :] = kept[0:7]
-        for done in (r - 1, r):
+        for c in range(4):
+            send(r, c, 0).start()
             if r % 2 == 1:
-                for c in range(4):
-                    send(done, c).start()
+                send(r - 1, c, 1).start()
+                send(r, c, 1).start()
     for r in range(4):
         for c in range(4):
-            send(r, c).wait()
+            send(r, c, 0).wait()
+            send(r, c, 1).wait()
 
 
 def edge_kernel(got_ref, edge_ref):
@@ -329,7 +334,7 @@
         out_specs=hbm(),
         scratch_shapes=[
             pltpu.VMEM((groups, ROWS, 128), jnp.float32),
-            pltpu.SemaphoreType.DMA((groups,)),
+            pltpu.SemaphoreType.DMA((2, groups)),
         ],
         compiler_params=PARAMS,
         cost_estimate=cost(2),

time: 61.6 us -> 61.7 us (level)
  no operation moved by 1% of the time
where the time goes in v8:
time: 61.7 us; the launch traced here: 61.5 us
  blocking collectives  19.5 us (32%)
  starting transfers between devices  16.9 us (27%)
  waiting for transfers between devices  10.2 us (17%)
  Pallas kernels  7.6 us (12%)
  matrix products  3.15 us (5%)
  local copies, waits for them, and re-layouts  2.82 us (5%)
  other arithmetic  0.96 us (2%)
    all_to_all x1, blocking collectives, shards(): lax.all_to_all(mixed, 'term', 0, 0, axis_index_groups=[order], tiled=True)  19.5 us
    all_to_all x1, starting transfers between devices, shards(): lax.all_to_all(sent, 'term', 0, 0, axis_index_groups=[order], tiled=True)  9.53 us
    all_to_all x1, waiting for transfers between devices, shards(): lax.all_to_all(sent, 'term', 0, 0, axis_index_groups=[order], tiled=True)  5.37 us
    ppermute x1, starting transfers between devices, shards(): coef = coefs(modes, lax.ppermute(edge, ('term', 'space'), passes), weights)  4.43 us
    ppermute x1, waiting for transfers between devices, shards(): beyond = lax.ppermute(edges(got), ('term', 'space'), passes + between)  3.54 us
    dot_general x1, matrix products, tables(): lax.dot_general(at.astype(jnp.float32), value, (((0,), (0,)), ((), ())),...  3.15 us
    ppermute x1, starting transfers between devices, shards(): beyond = lax.ppermute(edges(got), ('term', 'space'), passes + between)  2.97 us
    pallas_call x1, Pallas kernels, mix(): pl.pallas_call(mix_kernel, out_shape=f32(slots // (2 * PAIRS), BLOCK, 128...  2.46 us
  transfers between devices with their start and end apart: 3, of which 3 were waited for; matrix products, arithmetic and copies ran while one was open for 9% of the time, Pallas kernels for 4%

profile of v8, /device:TPU:16, one launch (start us, length us, event | category | flops | bytes accessed | tf_op | source)
XLA Modules:
  0.0 61.5 jit_solution(2734020383993411806)
XLA Ops:
  0.0 1.1 %copy-done.1 = f32[18,32,256]{2,1,0:T(8,128)S(1)} copy-done((f32[18,32,256]{2,1,0:T(8,128)S(1)}, f32[18,32,256]{2,1,0:T(8,128)}, u32[]{:S(2)}) %copy-start.1) | copy-done | bytes 589848
  1.1 1.8 %shard_map.64 = f32[16,88,128]{2,1,0:T(8,128)} custom-call(f32[18,32,256]{2,1,0:T(8,128)S(1)} %copy-done.1), custom_call_target="tpu_custom_call" | custom-call | bytes 6000000 | tf_op jit(solution)/shard_map/pallas_call | solution.py:330
  2.9 9.5 %all-to-all-start = ((f32[16,88,128]{2,1,0:T(8,128)}), f32[16,88,128]{2,1,0:T(8,128)S(1)}, u32[]{:S(2)}, u32[]{:S(2)}) async-start(f32[16,88,128]{2,1,0:T(8,128)} %shard_map.64), calls=%async_computation | async-start | bytes 1441792 | tf_op jit(solution)/shard_map/all_to_all | solution.py:452
  12.5 0.2 copy.14
  12.7 4.4 %collective-permute-start = (f32[11,256]{1,0:T(8,128)S(1)}, f32[11,256]{1,0:T(8,128)S(1)}, u32[]{:S(2)}, u32[]{:S(2)}) collective-permute-start(f32[11,256]{1,0:T(8,128)S(1)} %fusion.18), channel_id=1, source_target_pairs={{49,48},{48,49},{130,1},{1,130},{179,178},{178,179},{4,131},{131,4... | collective-permute-start | bytes 33800 | tf_op jit(solution)/shard_map/ppermute | solution.py:456
  17.3 0.6 gather_fusion
  18.0 0.3 select_reduce_fusion
  18.5 3.1 %fusion = f32[288,31]{0,1:T(8,128)S(1)} fusion(s32[2048]{0:T(1024)S(1)} %bitcast.7, f32[2048]{0:T(1024)S(1)} %convert_element_type.14, f32[2048]{0:T(1024)S(1)} %copy-done.5, s32[31]{0:T(128)S(1)} %iota_select_fusion, s32[2048]{0:T(1024)S(1)} %bitcast.6, pred[2048]{0:T(1024)(128)(4,1)S(1)} %get-tuple-element.22, pred[31]{0:T(512)(128)(4,1)S(1)} %get-tuple-element.28, ...), kind=kOutput, calls=%fused_computation.2 | convolution fusion | flops 220385280 | bytes 74810 | tf_op jit(solution)/shard_map/dot_general | solution.py:419
  21.6 0.1 copy.18
  21.7 0.1 reshape.52
  21.9 0.1 iota_compare_fusion.2
  22.1 0.2 select_reduce_fusion.1
  22.4 0.1 copy.20
  22.5 1.3 %collective-permute-done.edge_ref = f32[11,256]{1,0:T(8,128)S(1)} collective-permute-done((f32[11,256]{1,0:T(8,128)S(1)}, f32[11,256]{1,0:T(8,128)S(1)}, u32[]{:S(2)}, u32[]{:S(2)}) %collective-permute-start) | collective-permute-done | bytes 11296 | tf_op jit(solution)/shard_map/ppermute | solution.py:456
  23.8 0.3 broadcast_in_dim.145.weight_ref
  24.1 0.2 shard_map.65.coef_ref
  24.3 5.4 %all-to-all-done.got_ref = f32[16,88,128]{2,1,0:T(8,128)S(1)} async-done(((f32[16,88,128]{2,1,0:T(8,128)}), f32[16,88,128]{2,1,0:T(8,128)S(1)}, u32[]{:S(2)}, u32[]{:S(2)}) %all-to-all-start) | async-done | bytes 720928 | tf_op jit(solution)/shard_map/all_to_all | solution.py:452
  29.7 0.1 broadcast_in_dim.151.own_ref
  29.8 3.0 %collective-permute-start.1 = (f32[144,128]{1,0:T(8,128)S(1)}, f32[144,128]{1,0:T(8,128)S(1)}, u32[]{:S(2)}, u32[]{:S(2)}) collective-permute-start(f32[144,128]{1,0:T(8,128)S(1)} %shard_map.67), channel_id=1, source_target_pairs={{49,48},{48,49},{130,1},{1,130},{179,178},{178,179},{4,131},{131,4... | collective-permute-start | bytes 221192 | tf_op jit(solution)/shard_map/ppermute | solution.py:458
  32.8 2.1 %shard_map.66 = (f32[288,16,128]{2,1,0:T(8,128)S(1)}, f32[288,8,128]{2,1,0:T(8,128)S(1)}) custom-call(f32[288,128]{1,0:T(8,128)S(1)} %broadcast_in_dim.151.own_ref, f32[16,88,128]{2,1,0:T(8,128)S(1)} %all-to-all-done.got_ref, f32[11,16,128]{2,1,0:T(8,128)S(1)} %shard_map.65.coef_ref), custom_call_target="tpu_custom_call" | custom-call | bytes 12000000 | tf_op jit(solution)/shard_map/pallas_call | solution.py:368
  35.0 3.5 %collective-permute-done.1.edge_ref = f32[144,128]{1,0:T(8,128)S(1)} collective-permute-done((f32[144,128]{1,0:T(8,128)S(1)}, f32[144,128]{1,0:T(8,128)S(1)}, u32[]{:S(2)}, u32[]{:S(2)}) %collective-permute-start.1) | collective-permute-done | bytes 73760 | tf_op jit(solution)/shard_map/ppermute | solution.py:458
  38.5 2.5 %shard_map.68 = f32[16,72,128]{2,1,0:T(8,128)S(1)} custom-call(s32[1024]{0:T(1024)S(1)} %pad.9.place_ref, f32[288,128]{1,0:T(8,128)S(1)} %broadcast_in_dim.151.own_ref, f32[66,24,128]{2,1,0:T(8,128)S(1)} %broadcast_in_dim.145.weight_ref, f32[288,16,128]{2,1,0:T(8,128)S(1)} %get-tuple-element.19.diff_ref, f32[288,8,128]{2,1,0:T(8,128)S(1)} %get-tuple-element.20.start_ref, ...), custom_call_target="tpu_custom_call" | custom-call | bytes 15000000 | tf_op jit(solution)/shard_map/pallas_call | solution.py:380
  41.0 19.5 %all_to_all.10.got_ref = f32[16,72,128]{2,1,0:T(8,128)S(1)} all-to-all(f32[16,72,128]{2,1,0:T(8,128)S(1)} %shard_map.68), channel_id=1, replica_groups={{112,240,48,176,80,208,16,144,96,224,32,160,64,192,0,128},{113,241,49,1..., dimensions={0} | all-to-all | bytes 1179648 | tf_op jit(solution)/shard_map/all_to_all | solution.py:461
  60.5 1.0 %shard_map.69 = f32[18,32,256]{2,1,0:T(8,128)} custom-call(f32[16,72,128]{2,1,0:T(8,128)S(1)} %all_to_all.10.got_ref), custom_call_target="tpu_custom_call" | custom-call | bytes 3000000 | tf_op jit(solution)/shard_map/pallas_call | solution.py:397
  (28 shorter events, 0.5 us)
Async XLA Ops:
  0.0 17.3 %copy-start.4 = (s32[16]{0:T(128)S(1)}, s32[16]{0:T(128)}, u32[]{:S(2)}) copy-start(s32[16]{0:T(128)} %constant.52) | copy-start | bytes 196
  0.0 12.5 %copy-start = (f32[11,32,256]{2,1,0:T(8,128)S(1)}, f32[11,32,256]{2,1,0:T(8,128)}, u32[]{:S(2)}) copy-start(f32[11,32,256]{2,1,0:T(8,128)} %modes_ref) | copy-start | bytes 1081348
  0.0 1.1 %copy-start.1 = (f32[18,32,256]{2,1,0:T(8,128)S(1)}, f32[18,32,256]{2,1,0:T(8,128)}, u32[]{:S(2)}) copy-start(f32[18,32,256]{2,1,0:T(8,128)} %f_ref.1) | copy-start | bytes 1769476
  1.1 16.1 %copy-start.2 = (s32[2048,3]{0,1:T(4,128)S(1)}, s32[2048,3]{0,1:T(4,128)}, u32[]{:S(2)}) copy-start(s32[2048,3]{0,1:T(4,128)} %param.8) | copy-start | bytes 73732
  1.1 16.1 %copy-start.3 = (s32[288]{0:T(512)S(1)}, s32[288]{0:T(512)}, u32[]{:S(2)}) copy-start(s32[288]{0:T(512)} %param.10) | copy-start | bytes 3460
  1.1 17.3 %copy-start.5 = (f32[2048]{0:T(1024)S(1)}, f32[2048]{0:T(1024)}, u32[]{:S(2)}) copy-start(f32[2048]{0:T(1024)} %param.9) | copy-start | bytes 24580
  2.9 26.8 %all-to-all-start = ((f32[16,88,128]{2,1,0:T(8,128)}), f32[16,88,128]{2,1,0:T(8,128)S(1)}, u32[]{:S(2)}, u32[]{:S(2)}) async-start(f32[16,88,128]{2,1,0:T(8,128)} %shard_map.64), calls=%async_computation | async-start | bytes 1441792 | tf_op jit(solution)/shard_map/all_to_all | solution.py:452
  12.7 11.1 %collective-permute-start = (f32[11,256]{1,0:T(8,128)S(1)}, f32[11,256]{1,0:T(8,128)S(1)}, u32[]{:S(2)}, u32[]{:S(2)}) collective-permute-start(f32[11,256]{1,0:T(8,128)S(1)} %fusion.18), channel_id=1, source_target_pairs={{49,48},{48,49},{130,1},{1,130},{179,178},{178,179},{4,131},{131,4... | collective-permute-start | bytes 33800 | tf_op jit(solution)/shard_map/ppermute | solution.py:456
  29.8 8.7 %collective-permute-start.1 = (f32[144,128]{1,0:T(8,128)S(1)}, f32[144,128]{1,0:T(8,128)S(1)}, u32[]{:S(2)}, u32[]{:S(2)}) collective-permute-start(f32[144,128]{1,0:T(8,128)S(1)} %shard_map.67), channel_id=1, source_target_pairs={{49,48},{48,49},{130,1},{1,130},{179,178},{178,179},{4,131},{131,4... | collective-permute-start | bytes 221192 | tf_op jit(solution)/shard_map/ppermute | solution.py:458
